TPU v7x, 128 devices: a whole 4x4x4 slice. The times are simulated.
128 devices in a mesh: wn: 8 (over z_hi, y), sp: 16 (over z_lo, x, core).
Axes of the slice: x: 4, y: 4, z: 4 (z_hi: 2, z_lo: 2; z = z_hi * 2 + z_lo), core: 2. Of those that a mesh axis runs over, the one named last changes fastest.
Arguments:
- adjoint: float32 [3, 16, 512, 2048], P(None, None, 'wn', 'sp'), may hold values from -6 to 6
- base_flow: float32 [3, 16, 512, 2048], P(None, None, 'wn', 'sp'), may hold values from -6 to 6
- metric: float32 [512], P('wn'), may hold values from 0.25 to 2
- propagator: float32 [512, 512], replicated
- sensor_cell: int32 [16384], P(('wn', 'sp')), may hold values from 0 to 65535
- stream_stress: float32 [16384], P(('wn', 'sp')), may hold values from -6 to 6
- span_stress: float32 [16384], P(('wn', 'sp')), may hold values from -6 to 6
- sensor_count: int32 [128], P(('wn', 'sp')), may hold values from 32 to 128, as said below
Outputs:
- updated: float32 [3, 16, 512, 2048], P(None, None, 'wn', 'sp')
Inputs may be any that keep to these rules, and one draw needn't show every extreme that they name: `sensor_count`: live sensor slots of a device; the most is reached by some device.
All inputs are finite; a program needn't handle non-finite values.
Results may differ from a plain program's by a relative error of at most 0.00007.
Values sent between devices are 32-bit elements; how exact they have to be, the bound alone decides.
A program may use at most 128 MiB of HBM per device.

v0:
```python
import jax
import jax.numpy as jnp
from jax import lax
from jax.sharding import PartitionSpec as P

streamwise_scale = 0.5
spanwise_scale = 0.5
time_step = 0.25


def extended(cells, sides, width, closed):
    for axis, dim in sides:
        count = lax.axis_size(axis)
        ends = count if closed else count - 1
        head = lax.slice_in_dim(cells, 0, width, axis=dim)
        tail = lax.slice_in_dim(cells, cells.shape[dim] - width, cells.shape[dim], axis=dim)
        cells = jnp.concatenate(
            [
                lax.ppermute(tail, axis, [(i, (i + 1) % count) for i in range(ends)]),
                cells,
                lax.ppermute(head, axis, [((i + 1) % count, i) for i in range(ends)]),
            ],
            axis=dim,
        )
    return cells


def tendency(adjoint, base_flow, gradients):
    advect = (
        base_flow[0] * gradients[0][:3]
        + base_flow[1] * gradients[1][:3]
        + base_flow[2] * gradients[2][:3]
    )
    stretch = jnp.stack(
        [
            jnp.sum(adjoint * gradients[0][3:], 0),
            jnp.sum(adjoint * gradients[1][3:], 0),
            jnp.sum(adjoint * gradients[2][3:], 0),
        ]
    )
    return adjoint + time_step * (advect - stretch)


def derivatives(stacked, metric):
    along_y = extended(stacked, (("wn", 2),), 1, False)
    along_z = extended(stacked, (("sp", 3),), 1, True)
    grad_x = (jnp.roll(stacked, -1, 1) - jnp.roll(stacked, 1, 1)) * streamwise_scale
    grad_y = (along_y[:, :, 2:, :] - along_y[:, :, :-2, :]) * metric[None, None, :, None]
    grad_z = (along_z[:, :, :, 2:] - along_z[:, :, :, :-2]) * spanwise_scale
    return (grad_x, grad_y, grad_z)


def per_device(
    adjoint, base_flow, metric, propagator, sensor_cell, stream_stress, span_stress, sensor_count
):
    planes = adjoint.shape[1]
    cells_y = adjoint.shape[2]
    cells_z = adjoint.shape[3]
    width_z = cells_z * lax.axis_size("sp")
    depth_index = lax.axis_index("wn")
    stacked = jnp.concatenate([adjoint, base_flow], 0)
    forcing = tendency(adjoint, base_flow, derivatives(stacked, metric))
    slot_count = sensor_cell.shape[0]
    alive_slot = jnp.arange(slot_count, dtype=jnp.int32) < sensor_count[0]
    stream_part = jnp.where(alive_slot, stream_stress, 0.0)
    span_part = jnp.where(alive_slot, span_stress, 0.0)
    wall_side = sensor_cell // (planes * width_z)
    remainder = sensor_cell % (planes * width_z)
    wall_side, plane_x, global_z = (wall_side, remainder // width_z, remainder % width_z)
    target = (wall_side * planes + plane_x) * width_z + global_z
    plane_sum = jnp.zeros((2, 2 * planes * width_z), jnp.float32)
    plane_sum = plane_sum.at[:, target].add(jnp.stack([stream_part, span_part]))
    plane_sum = plane_sum.reshape(2, 2, planes, width_z)
    shared = lax.psum_scatter(plane_sum, "sp", scatter_dimension=3, tiled=True)
    walls = lax.psum(shared, "wn")
    nothing = jnp.zeros((planes, cells_z), jnp.float32)
    lower = jnp.stack([walls[0, 0], nothing, walls[1, 0]])
    upper = jnp.stack([walls[0, 1], nothing, walls[1, 1]])
    row_pos = jnp.arange(cells_y, dtype=jnp.int32)
    lower_mask = ((row_pos == 1) & (depth_index == 0)).astype(jnp.float32)
    upper_mask = ((row_pos == cells_y - 2) & (depth_index == lax.axis_size("wn") - 1)).astype(
        jnp.float32
    )
    forcing = forcing + (
        lower[:, :, None, :] * lower_mask[None, None, :, None]
        + upper[:, :, None, :] * upper_mask[None, None, :, None]
    )
    own_rows = lax.dynamic_slice_in_dim(propagator, depth_index * cells_y, cells_y, 0)
    return jnp.einsum(
        "yk,cxkz->cxyz",
        own_rows,
        lax.all_gather(forcing, "wn", axis=2, tiled=True),
        precision=lax.Precision.HIGHEST,
    )


def solution(mesh):
    placed = (
        P(None, None, "wn", "sp"),
        P(None, None, "wn", "sp"),
        P("wn"),
        P(),
        P(("wn", "sp")),
        P(("wn", "sp")),
        P(("wn", "sp")),
        P(("wn", "sp")),
    )
    return jax.shard_map(
        per_device, mesh=mesh, in_specs=placed, out_specs=P(None, None, "wn", "sp"), check_vma=False
    )
```

profile of v0, /device:TPU:1, one launch (start us, length us, event | category | flops | bytes accessed | tf_op | source)
XLA Modules:
  0.0 337.3 jit_solution(7970447104922733406)
XLA Ops:
  6.5 1.7 constant_dynamic-update-slice_fusion.1
  8.2 0.3 copy-done.6
  8.5 0.1 constant_dynamic-update-slice_fusion
  8.6 3.7 %fusion.25 = (f32[6,16,64,1]{3,2,1,0:T(8,128)}, f32[6,16,64,1]{3,2,1,0:T(8,128)}) fusion(f32[6,16,64,128]{3,2,1,0:T(8,128)S(1)} %constant_dynamic-update-slice_fusion), kind=kLoop, calls=%fused_computation.65 | loop fusion | bytes 98304 | tf_op jit(solution)/shard_map/slice | solution.py:15
  12.4 3.1 copy.11
  15.5 1.4 collective-permute-start.2
  16.9 3.0 copy.13
  19.9 1.2 collective-permute-start.3
  21.1 1.8 fusion.24
  23.0 1.3 collective-permute-start
  24.2 4.6 %collective-permute-start.1 = (f32[6,16,1,128]{3,2,1,0:T(1,128)}, f32[6,16,1,128]{3,2,1,0:T(1,128)}, u32[]{:S(2)}, u32[]{:S(2)}) collective-permute-start(f32[6,16,1,128]{3,2,1,0:T(1,128)} %get-tuple-element.15), channel_id=1, source_target_pairs={{0,16},{16,32},{32,48},{48,64},{64,80},{80,96},{96,112},{1,17},{17... | collective-permute-start | bytes 147464 | tf_op jit(solution)/shard_map/ppermute | solution.py:19
  29.5 0.1 copy.15
  29.7 14.2 %scatter_custom_fusion = f32[2,65536]{0,1:T(8,128)} fusion(s32[128]{0:T(128)S(1)} %compare_select_fusion, f32[128,2]{1,0:T(8,128)S(1)} %copy.15, f32[]{:T(128)} %constant.59.clone.1), kind=kCustom, calls=%fused_computation.1 | custom fusion | flops 256 | bytes 524292 | tf_op jit(solution)/shard_map/scatter-add | solution.py:72
  43.9 20.1 %copy.16 = f32[2,2,16,2048]{3,2,1,0:T(8,128)} copy(f32[2,2,16,2048]{0,3,2,1:T(8,128)} %bitcast.35) | data formatting | bytes 1048576 | tf_op jit(solution)/shard_map/reshape | solution.py:73
  64.0 0.2 all-gather.2.cloned.1.call-start
  64.3 6.3 %fusion.23 = (f32[6,15,64,128]{3,2,1,0:T(8,128)}, f32[6,15,64,128]{3,2,1,0:T(8,128)}) fusion(f32[6,16,64,128]{3,2,1,0:T(8,128)} %copy-done.1), kind=kLoop, calls=%fused_computation.63 | loop fusion | bytes 11796480 | tf_op jit(solution)/shard_map/jit(_roll_static)/slice | solution.py:47
  70.6 1.0 fusion.22
  71.6 1.1 slice_bitcast_fusion.2
  72.7 5.4 %fusion.6 = f32[6,16,64,128]{3,2,1,0:T(8,128)} fusion(f32[6,1,64,128]{3,2,1,0:T(8,128)S(1)} %get-tuple-element.9, f32[6,15,64,128]{3,2,1,0:T(8,128)} %get-tuple-element.11, f32[6,15,64,128]{3,2,1,0:T(8,128)} %get-tuple-element.10, f32[6,1,64,128]{3,2,1,0:T(8,128)S(1)} %get-tuple-element.8), kind=kLoop, calls=%fused_computation.12 | loop fusion | flops 3145728 | bytes 9437184 | tf_op jit(solution)/shard_map/mul | solution.py:47
  78.1 0.1 pad.4.clone
  78.2 3.0 copy.12
  81.2 3.1 copy.14
  84.3 8.8 %fusion.5 = (f32[6,16,64,128]{3,2,1,0:T(8,128)S(1)}, f32[6,16,64,128]{3,2,1,0:T(8,128)S(1)}) fusion(f32[6,16,64,128]{3,2,1,0:T(8,128)} %copy-done.1, f32[6,16,1,128]{3,2,1,0:T(1,128)} %collective-permute-done.1, f32[6,16,1,128]{3,2,1,0:T(1,128)} %collective-permute-done, f32[64]{0:T(128)S(1)} %copy-done.7, f32[6,16,64,1]{3,2,1,0:T(8,128)} %copy.14, ...), kind=kLoop, calls=%fused_computation.9 | loop fusion | flops 6291456 | bytes 9584896 | tf_op jit(solution)/shard_map/mul | solution.py:48
  93.1 1.7 copy-done.4
  94.8 1.1 copy-done.5
  95.9 2.0 fusion.9
  97.9 27.7 %reduce-scatter.2.cloned.1.call-done = f32[2,2,16,128]{3,2,1,0:T(8,128)} async-done(((f32[2,2,16,2048]{3,2,1,0:T(8,128)}), f32[2,2,16,128]{3,2,1,0:T(8,128)}) %reduce-scatter.2.cloned.1.call-update) | async-done | bytes 32784 | tf_op jit(solution)/shard_map/reduce_scatter | solution.py:74
  125.5 35.6 %psum.7 = f32[2,2,16,128]{3,2,1,0:T(8,128)S(1)} all-reduce(f32[2,2,16,128]{3,2,1,0:T(8,128)} %reduce-scatter.2.cloned.1.call-done), channel_id=1, replica_groups=mesh['wn'=8,'sp'=16] {'wn'}, use_global_device_ids=true, to_apply=%region_5.6 | all-reduce | flops 8192 | bytes 65536 | tf_op jit(solution)/shard_map/psum | solution.py:75
  161.1 0.1 pad_maximum_fusion.4
  161.2 5.5 %fusion.14 = f32[3,16,64,128]{3,2,1,0:T(8,128)} fusion(f32[3,16,64,128]{3,2,1,0:T(8,128)S(1)} %copy-done.2, f32[6,16,64,128]{3,2,1,0:T(8,128)} %copy-done.5, f32[6,16,64,128]{3,2,1,0:T(8,128)} %copy-done.4, f32[6,16,64,128]{3,2,1,0:T(8,128)} %fusion.6, f32[1,16,64,128]{3,2,1,0:T(8,128)} %bitcast.38, f32[1,16,64,128]{3,2,1,0:T(8,128)} %bitcast.37, ...), kind=kLoop, calls=%fused_computation.24 | loop fusion | flops 5505024 | bytes 11059712 | tf_op jit(solution)/shard_map/add | solution.py:84
  166.7 151.4 %all-gather.2.cloned.1.call-done = f32[3,16,512,128]{3,2,1,0:T(8,128)} async-done(((f32[3,16,64,128]{3,2,1,0:T(8,128)}), f32[3,16,512,128]{3,2,1,0:T(8,128)}) %all-gather.2.cloned.1.call-update) | async-done | bytes 12582928 | tf_op jit(solution)/shard_map/all_gather | solution.py:92
  318.2 12.3 %convolution_bitcast_fusion = f32[3,16,64,128]{3,2,1,0:T(8,128)} fusion(f32[3,16,512,128]{3,2,1,0:T(8,128)} %all-gather.2.cloned.1.call-done, f32[512,512]{1,0:T(8,128)S(1)} %copy-done, s32[]{:T(128)S(6)} %select_n.39), kind=kOutput, calls=%fused_computation.28 | convolution fusion | flops 2415919104 | bytes 14286852 | tf_op jit(solution)/shard_map/yk,cxkz->cxyz/dot_general | solution.py:89
  (31 shorter events, 0.1 us)
Async XLA Ops:
  6.5 311.6 %copy-start = (f32[512,512]{1,0:T(8,128)S(1)}, f32[512,512]{1,0:T(8,128)}, u32[]{:S(2)}) copy-start(f32[512,512]{1,0:T(8,128)} %param.11) | copy-start | bytes 3145732
  6.5 2.0 copy-start.6
  6.5 119.0 %reduce-scatter.2.cloned.1.call-start = ((), (), s32[]{:S(2)}) async-start(), calls=%async_computation.1 | async-start | bytes 557056 | tf_op jit(solution)/shard_map/reduce_scatter | solution.py:74
  8.6 3.8 %copy-start.1 = (f32[6,16,64,128]{3,2,1,0:T(8,128)}, f32[6,16,64,128]{3,2,1,0:T(8,128)S(1)}, u32[]{:S(2)}) copy-start(f32[6,16,64,128]{3,2,1,0:T(8,128)S(1)} %constant_dynamic-update-slice_fusion) | copy-start | bytes 9437188
  12.4 17.1 %copy-start.8 = (f32[128]{0:T(128)S(1)}, f32[128]{0:T(128)}, u32[]{:S(2)}) copy-start(f32[128]{0:T(128)} %param.13) | copy-start | bytes 1540
  12.4 17.1 %copy-start.9 = (f32[128]{0:T(128)S(1)}, f32[128]{0:T(128)}, u32[]{:S(2)}) copy-start(f32[128]{0:T(128)} %param.14) | copy-start | bytes 1540
  12.4 17.3 %copy-start.10 = (s32[128]{0:T(128)S(1)}, s32[128]{0:T(128)}, u32[]{:S(2)}) copy-start(s32[128]{0:T(128)} %param.12) | copy-start | bytes 1540
  15.5 62.7 %collective-permute-start.2 = (f32[6,16,64,1]{2,1,3,0:T(8,128)}, f32[6,16,64,1]{2,1,3,0:T(8,128)}, u32[]{:S(2)}, u32[]{:S(2)}) collective-permute-start(f32[6,16,64,1]{2,1,3,0:T(8,128)} %copy.11), channel_id=1, source_target_pairs={{1,0},{2,1},{3,2},{4,3},{5,4},{6,5},{7,6},{8,7},{9,8},{10,9},{11,1... | collective-permute-start | bytes 73736 | tf_op jit(solution)/shard_map/ppermute | solution.py:21
  19.9 61.2 %collective-permute-start.3 = (f32[6,16,64,1]{2,1,3,0:T(8,128)}, f32[6,16,64,1]{2,1,3,0:T(8,128)}, u32[]{:S(2)}, u32[]{:S(2)}) collective-permute-start(f32[6,16,64,1]{2,1,3,0:T(8,128)} %copy.13), channel_id=1, source_target_pairs={{0,1},{1,2},{2,3},{3,4},{4,5},{5,6},{6,7},{7,8},{8,9},{9,10},{10,1... | collective-permute-start | bytes 73736 | tf_op jit(solution)/shard_map/ppermute | solution.py:19
  23.0 61.3 %collective-permute-start = (f32[6,16,1,128]{3,2,1,0:T(1,128)}, f32[6,16,1,128]{3,2,1,0:T(1,128)}, u32[]{:S(2)}, u32[]{:S(2)}) collective-permute-start(f32[6,16,1,128]{3,2,1,0:T(1,128)} %get-tuple-element.14), channel_id=1, source_target_pairs={{16,0},{32,16},{48,32},{64,48},{80,64},{96,80},{112,96},{17,1},{33... | collective-permute-start | bytes 147464 | tf_op jit(solution)/shard_map/ppermute | solution.py:21
  24.2 60.0 %collective-permute-start.1 = (f32[6,16,1,128]{3,2,1,0:T(1,128)}, f32[6,16,1,128]{3,2,1,0:T(1,128)}, u32[]{:S(2)}, u32[]{:S(2)}) collective-permute-start(f32[6,16,1,128]{3,2,1,0:T(1,128)} %get-tuple-element.15), channel_id=1, source_target_pairs={{0,16},{16,32},{32,48},{48,64},{64,80},{80,96},{96,112},{1,17},{17... | collective-permute-start | bytes 147464 | tf_op jit(solution)/shard_map/ppermute | solution.py:19
  64.0 254.1 %all-gather.2.cloned.1.call-start = ((), (), s32[]{:S(2)}) async-start(), calls=%async_computation.2 | async-start | bytes 14155776 | tf_op jit(solution)/shard_map/all_gather | solution.py:92
  78.2 6.1 %copy-start.7 = (f32[64]{0:T(128)S(1)}, f32[64]{0:T(128)}, u32[]{:S(2)}) copy-start(f32[64]{0:T(128)} %param.10) | copy-start | bytes 772
  84.3 11.6 %copy-start.2 = (f32[3,16,64,128]{3,2,1,0:T(8,128)S(1)}, f32[3,16,64,128]{3,2,1,0:T(8,128)}, u32[]{:S(2)}) copy-start(f32[3,16,64,128]{3,2,1,0:T(8,128)} %param.8) | copy-start | bytes 4718596
  84.3 11.6 %copy-start.3 = (f32[6,16,64,128]{3,2,1,0:T(8,128)S(1)}, f32[6,16,64,128]{3,2,1,0:T(8,128)}, u32[]{:S(2)}) copy-start(f32[6,16,64,128]{3,2,1,0:T(8,128)} %fusion.6) | copy-start | bytes 9437188
  93.1 1.7 copy-start.4
  93.1 2.8 copy-start.5
Sparse Core Ops, SparseCore 0:
  64.2 61.3 reduce-scatter.1
  166.9 151.2 all-gather.1
where the time goes:
time: 338 us; the launch traced here: 337 us
  waiting for transfers between devices  179 us (53%)
  local copies, waits for them, and re-layouts  51.5 us (15%)
  other arithmetic  35.9 us (11%)
  blocking collectives  35.6 us (11%)
  between operations  14.2 us (4%)
  matrix products  12.3 us (4%)
  starting transfers between devices  8.71 us (3%)
    all_gather x1, waiting for transfers between devices, per_device(): lax.all_gather(forcing, 'wn', axis=2, tiled=True)  151 us
    psum x1, blocking collectives, per_device(): walls = lax.psum(shared, 'wn')  35.6 us
    reduce_scatter x1, waiting for transfers between devices, per_device(): shared = lax.psum_scatter(plane_sum, 'sp', scatter_dimension=3, tiled=True)  27.7 us
    reshape x1, local copies, waits for them, and re-layouts, per_device(): plane_sum = plane_sum.reshape(2, 2, planes, width_z)  20.1 us
    scatter-add x1, other arithmetic, per_device(): plane_sum = plane_sum.at[:, target].add(jnp.stack([stream_part, span_part]))  14.2 us
    dot_general x1, matrix products, per_device(): jnp.einsum('yk,cxkz->cxyz', own_rows, lax.all_gather(forcing, 'wn', axis=...  12.3 us
    mul x1, other arithmetic, derivatives(): (along_y[:, :, 2:, :] - along_y[:, :, :-2, :]) * metric[None, None, :, None]  8.77 us
    slice x3, local copies, waits for them, and re-layouts, extended(): head = lax.slice_in_dim(cells, 0, width, axis=dim)  8.65 us
  transfers between devices with their start and end apart: 6, of which 2 were waited for; matrix products, arithmetic and copies ran while one was open for 21% of the time, Pallas kernels for 0%

commit v1 on v0

v1 whole, which is shorter than its diff:
```python
import jax
import jax.numpy as jnp
from jax import lax
from jax.experimental import pallas as pl
from jax.experimental.pallas import tpu as pltpu
from jax.sharding import PartitionSpec as P

MESH = pl.DeviceIdType.MESH
BF16 = jnp.bfloat16
F32 = jnp.float32

NF = 6
PAD = 8
WN = 8
SP = 16


def kernel(
    adj_ref, base_ref, metric_ref, prop_ref, cell_ref, stream_ref, span_ref, count_ref,
    out_ref,
    fld, yh_out, yh_in, zh_out, zh_in, zh, met, send, cols, cols3, prop, prop3, rows_out,
    msg, slots, pick_rows, pick_cells, wall_part, wall_in,
    load_sem, y_send, y_recv, z_send, z_recv, f_send, f_recv, u_send, u_recv, own_sem,
    s_send, s_recv, w_send, w_recv,
):
    planes = out_ref.shape[1]
    ny = out_ref.shape[2]
    nz = out_ref.shape[3]
    tall = ny + 2 * PAD
    blocks = ny // 8
    w = lax.axis_index("wn")
    s = lax.axis_index("sp")
    lane = lax.broadcasted_iota(jnp.int32, (8, nz), 1)

    def peer(j):
        i = j // 2
        dy = (2 - i + 3 * (i // 2) - 2 * (i // 3)) % 4
        return ((w // 4 + 1 - j % 2) % 2) * 4 + (w + dy) % 4

    loads = [
        pltpu.make_async_copy(adj_ref, fld.at[pl.ds(0, 3 * planes), pl.ds(PAD, ny), :], load_sem.at[0]),
        pltpu.make_async_copy(base_ref, fld.at[pl.ds(3 * planes, 3 * planes), pl.ds(PAD, ny), :], load_sem.at[1]),
        pltpu.make_async_copy(prop_ref, prop, load_sem.at[2]),
    ]
    for load in loads:
        load.start()

    barrier = pltpu.get_barrier_semaphore()
    for j in range(WN - 1):
        pl.semaphore_signal(barrier, inc=1, device_id=(peer(j), s), device_id_type=MESH)
    for o in range(1, SP):
        pl.semaphore_signal(barrier, inc=1, device_id=(w, (s + o) % SP), device_id_type=MESH)

    alive = lax.broadcasted_iota(jnp.int32, (1, nz), 1) < count_ref[0]
    msg[...] = jnp.concatenate(
        [
            cell_ref[...].astype(F32),
            jnp.where(alive, stream_ref[...], 0.0),
            jnp.where(alive, span_ref[...], 0.0),
            jnp.zeros((5, nz), F32),
        ],
        0,
    )
    here = lax.broadcasted_iota(jnp.int32, (ny, ny), 0) == lax.broadcasted_iota(jnp.int32, (ny, ny), 1)
    column = jnp.sum(jnp.where(here, jnp.broadcast_to(metric_ref[...], (ny, ny)), 0.0), 1, keepdims=True)
    met[...] = jnp.broadcast_to(column, (ny, nz))

    loads[0].wait()
    loads[1].wait()
    flat = fld.reshape(NF * planes * tall, nz)
    yh_out[0] = flat[pl.ds(PAD + ny - 1, NF * planes, stride=tall), :]
    yh_out[1] = flat[pl.ds(PAD, NF * planes, stride=tall), :]

    def pack(r, carry):
        at = pl.multiple_of(r * 8, 8)
        for half in range(2):
            edge = jnp.zeros((8, nz), F32)
            for i in range(3 * planes):
                tile = fld[half * 3 * planes + i, pl.ds(PAD + at, 8), :]
                edge = jnp.where(lane // 2 == i, pltpu.roll(tile, 2 * i + 1, 1), edge)
            zh_out[half, pl.ds(at, 8), :] = edge
        return carry

    lax.fori_loop(0, blocks, pack, 0)

    pl.semaphore_wait(barrier, WN - 1 + SP - 1)

    halo = []
    for side in range(2):
        step = 1 - 2 * side
        halo.append(pltpu.make_async_remote_copy(
            zh_out, zh_in.at[side], z_send.at[side], z_recv.at[side],
            device_id=(w, (s + step) % SP), device_id_type=MESH))
        halo.append(pltpu.make_async_remote_copy(
            yh_out.at[side], yh_in.at[side], y_send.at[side], y_recv.at[side],
            device_id=((w + step) % WN, s), device_id_type=MESH))
    for copy in halo:
        copy.start()
    slot_copies = [
        pltpu.make_async_remote_copy(
            msg, slots.at[o], s_send.at[o], s_recv.at[o],
            device_id=(w, (s + o) % SP), device_id_type=MESH)
        for o in range(1, SP)
    ]
    for copy in slot_copies:
        copy.start()
    slots[0] = msg[...]

    depth = prop.shape[1]
    loads[2].wait()
    whole = prop[...]
    high = whole.astype(BF16)
    prop3[:, pl.ds(0, depth)] = high
    prop3[:, pl.ds(depth, depth)] = (whole - high.astype(F32)).astype(BF16)
    prop3[:, pl.ds(2 * depth, depth)] = high

    for copy in halo:
        copy.wait()
    flat[pl.ds(PAD - 1, NF * planes, stride=tall), :] = jnp.where(w == 0, 0.0, yh_in[0])
    flat[pl.ds(PAD + ny, NF * planes, stride=tall), :] = jnp.where(w == WN - 1, 0.0, yh_in[1])
    odd = lax.broadcasted_iota(jnp.int32, (ny, nz), 1) % 2 == 1
    for half in range(2):
        zh[half] = jnp.where(odd, zh_in[1, half], pltpu.roll(zh_in[0, half], 2, 1))

    def forcing(x, put):
        ahead, behind = (x + 1) % planes, (x + planes - 1) % planes

        def block(r, carry):
            at = pl.multiple_of(r * 8, 8)
            m = met[pl.ds(at, 8), :]
            mid, gx, gy, gz = [], [], [], []
            for f in range(NF):
                t = f * planes + x
                here = fld[t, pl.ds(PAD + at, 8), :]
                mid.append(here)
                gx.append((fld[f * planes + ahead, pl.ds(PAD + at, 8), :]
                           - fld[f * planes + behind, pl.ds(PAD + at, 8), :]) * 0.5)
                gy.append((fld[t, pl.ds(PAD + 1 + at, 8), :] - fld[t, pl.ds(PAD - 1 + at, 8), :]) * m)
                ends = pltpu.roll(zh[f // 3, pl.ds(at, 8), :], nz - 2 - 2 * ((f % 3) * planes + x), 1)
                gz.append((jnp.where(lane == nz - 1, ends, pltpu.roll(here, nz - 1, 1))
                           - jnp.where(lane == 0, ends, pltpu.roll(here, 1, 1))) * 0.5)
            for c in range(3):
                advect = mid[3] * gx[c] + mid[4] * gy[c] + mid[5] * gz[c]
                grad = (gx, gy, gz)[c]
                stretch = mid[0] * grad[3] + mid[1] * grad[4] + mid[2] * grad[5]
                put(at, c, mid[c] + 0.25 * (advect - stretch))
            return carry

        lax.fori_loop(0, blocks, block, 0)

    def columns_copy(k, j):
        return pltpu.make_async_remote_copy(
            send.at[k, j], cols.at[k, pl.ds(pl.multiple_of(w * ny, ny), ny), :],
            f_send.at[k, j], f_recv.at[k, j],
            device_id=(peer(j), s), device_id_type=MESH)

    def chunk(k):
        def to(j, carry):
            def put(at, c, value):
                send[k, j, pl.ds(at, 8), pl.ds(c * nz, nz)] = value

            forcing(2 * peer(j) + k, put)
            columns_copy(k, j).start()
            return carry

        lax.fori_loop(0, WN - 1, to, 0)

        def put(at, c, value):
            cols[k, pl.ds(pl.multiple_of(w * ny, ny) + at, 8), pl.ds(c * nz, nz)] = value

        forcing(2 * w + k, put)

    chunk(0)

    for copy in slot_copies:
        copy.wait()
    for i in range(SP):
        got = slots[i]
        cell = got[0:1].astype(jnp.int32)
        side = cell // (planes * nz * SP)
        left = cell % (planes * nz * SP)
        key = (left // (nz * SP)) * 2 + side
        spot = left % (nz * SP) - s * nz
        row = lax.broadcasted_iota(jnp.int32, (4 * planes, nz), 0)
        parts = [got[1:2], got[2:3]]
        for p in range(3):
            tops = [v.astype(BF16).astype(F32) for v in parts]
            parts = [v - t for v, t in zip(parts, tops)]
            pick = jnp.where(row // 2 == key, jnp.where(row % 2 == 0, tops[0], tops[1]), 0.0)
            pick_rows[pl.ds(p * 4 * planes, 4 * planes), pl.ds(i * nz, nz)] = pick.astype(BF16)
        cells = lax.broadcasted_iota(jnp.int32, (nz, nz), 0)
        pick_cells[:, pl.ds(i * nz, nz)] = jnp.where(cells == spot, 1.0, 0.0).astype(BF16)
    summed = lax.dot_general(
        pick_rows[...], pick_cells[...], (((1,), (1,)), ((), ())), preferred_element_type=F32)
    n = 4 * planes
    wall_part[...] = summed[0:n] + summed[n:2 * n] + summed[2 * n:3 * n]
    wall_copies = [
        pltpu.make_async_remote_copy(
            wall_part.at[pl.ds(pl.multiple_of(peer(j) * 8, 8), 8), :], wall_in.at[j],
            w_send.at[j], w_recv.at[j], device_id=(peer(j), s), device_id_type=MESH)
        for j in range(WN - 1)
    ]
    for copy in wall_copies:
        copy.start()
    wall_in[WN - 1] = wall_part[pl.ds(pl.multiple_of(w * 8, 8), 8), :]

    chunk(1)

    for copy in wall_copies:
        copy.wait()
    walls = wall_in[0]
    for j in range(1, WN):
        walls = walls + wall_in[j]

    def rows_copy(k, j):
        to = peer(j)
        return pltpu.make_async_remote_copy(
            rows_out.at[k, :, pl.ds(pl.multiple_of(to * ny, ny), ny), :], out_ref.at[:, 2 * w + k],
            u_send.at[k, j], u_recv.at[k, j], device_id=(to, s), device_id_type=MESH)

    own = []
    for k in range(2):
        for j in range(WN - 1):
            columns_copy(k, j).wait_recv()
        for side, y in ((0, 1), (1, depth - 2)):
            for comp, c in ((0, 0), (1, 2)):
                at = k * 4 + side * 2 + comp
                spot = (k, pl.ds(y, 1), pl.ds(c * nz, nz))
                cols[spot] = cols[spot] + walls[at:at + 1]
        whole = cols[k]
        high = whole.astype(BF16)
        cols3[pl.ds(0, depth), :] = high
        cols3[pl.ds(depth, depth), :] = high
        cols3[pl.ds(2 * depth, depth), :] = (whole - high.astype(F32)).astype(BF16)
        updated = jnp.dot(prop3[...], cols3[...], preferred_element_type=F32)
        for c in range(3):
            rows_out[k, c] = updated[:, c * nz:(c + 1) * nz]
        for j in range(WN - 1):
            rows_copy(k, j).start()
        copy = pltpu.make_async_copy(
            rows_out.at[k, :, pl.ds(pl.multiple_of(w * ny, ny), ny), :], out_ref.at[:, 2 * w + k],
            own_sem.at[k])
        copy.start()
        own.append(copy)
    for k in range(2):
        for j in range(WN - 1):
            columns_copy(k, j).wait_send()
            rows_copy(k, j).wait()
        own[k].wait()


def per_device(
    adjoint, base_flow, metric, propagator, sensor_cell, stream_stress, span_stress, sensor_count
):
    comps, planes, ny, nz = adjoint.shape
    depth = propagator.shape[0]
    vmem = pl.BlockSpec(memory_space=pltpu.VMEM)
    anywhere = pl.BlockSpec(memory_space=pl.ANY)
    dma = pltpu.SemaphoreType.DMA
    return pl.pallas_call(
        kernel,
        name="substep",
        out_shape=jax.ShapeDtypeStruct(adjoint.shape, F32),
        in_specs=[anywhere, anywhere, vmem, anywhere, vmem, vmem, vmem,
                  pl.BlockSpec(memory_space=pltpu.SMEM)],
        out_specs=anywhere,
        scratch_shapes=[
            pltpu.VMEM((NF * planes, ny + 2 * PAD, nz), F32),
            pltpu.VMEM((2, NF * planes, nz), F32),
            pltpu.VMEM((2, NF * planes, nz), F32),
            pltpu.VMEM((2, ny, nz), F32),
            pltpu.VMEM((2, 2, ny, nz), F32),
            pltpu.VMEM((2, ny, nz), F32),
            pltpu.VMEM((ny, nz), F32),
            pltpu.VMEM((2, WN - 1, ny, comps * nz), F32),
            pltpu.VMEM((2, depth, comps * nz), F32),
            pltpu.VMEM((3 * depth, comps * nz), BF16),
            pltpu.VMEM((depth, depth), F32),
            pltpu.VMEM((depth, 3 * depth), BF16),
            pltpu.VMEM((2, comps, depth, nz), F32),
            pltpu.VMEM((8, nz), F32),
            pltpu.VMEM((SP, 8, nz), F32),
            pltpu.VMEM((12 * planes, SP * nz), BF16),
            pltpu.VMEM((nz, SP * nz), BF16),
            pltpu.VMEM((4 * planes, nz), F32),
            pltpu.VMEM((WN, 8, nz), F32),
            dma((3,)),
            dma((2,)), dma((2,)), dma((2,)), dma((2,)),
            dma((2, WN - 1)), dma((2, WN - 1)), dma((2, WN - 1)), dma((2, WN - 1)),
            dma((2,)),
            dma((SP,)), dma((SP,)), dma((WN - 1,)), dma((WN - 1,)),
        ],
        compiler_params=pltpu.CompilerParams(
            collective_id=0, has_side_effects=True, vmem_limit_bytes=48 << 20),
    )(
        adjoint.reshape(comps * planes, ny, nz),
        base_flow.reshape(comps * planes, ny, nz),
        metric.reshape(1, ny),
        propagator,
        sensor_cell.reshape(1, nz),
        stream_stress.reshape(1, nz),
        span_stress.reshape(1, nz),
        sensor_count,
    )


def solution(mesh):
    placed = (
        P(None, None, "wn", "sp"),
        P(None, None, "wn", "sp"),
        P("wn"),
        P(),
        P(("wn", "sp")),
        P(("wn", "sp")),
        P(("wn", "sp")),
        P(("wn", "sp")),
    )
    return jax.shard_map(
        per_device, mesh=mesh, in_specs=placed, out_specs=P(None, None, "wn", "sp"), check_vma=False
    )
```

time: 338 us -> 60.9 us (0.18)
  waiting for transfers between devices: 179 us -> 0 us
  Pallas kernels: 0 us -> 52.2 us
  local copies, waits for them, and re-layouts: 51.5 us -> 7.8 us
  other arithmetic: 35.9 us -> 0 us
  blocking collectives: 35.6 us -> 0 us
  between operations: 14.2 us -> 0.67 us
  matrix products: 12.3 us -> 0 us
  starting transfers between devices: 8.71 us -> 0 us
    all_gather x1 -> x0, waiting for transfers between devices: 151 us -> none  [per_device(): lax.all_gather(forcing, 'wn', axis=2, tiled=True)]
    pallas_call x0 -> x1, Pallas kernels: none -> 52.2 us  [per_device(): pl.pallas_call(kernel, name='substep', out_shape=jax.ShapeDtypeStruct(adj...]
    psum x1 -> x0, blocking collectives: 35.6 us -> none  [per_device(): walls = lax.psum(shared, 'wn')]
    reduce_scatter x1 -> x0, waiting for transfers between devices: 27.7 us -> none  [per_device(): shared = lax.psum_scatter(plane_sum, 'sp', scatter_dimension=3, tiled=True)]
    reshape x1 -> x0, local copies, waits for them, and re-layouts: 20.1 us -> none  [per_device(): plane_sum = plane_sum.reshape(2, 2, planes, width_z)]
    slice x6 -> x0, local copies, waits for them, and re-layouts: 19 us -> none  [the longest x3 8.65 us: extended(): head = lax.slice_in_dim(cells, 0, width, axis=dim)]
    scatter-add x1 -> x0, other arithmetic: 14.2 us -> none  [per_device(): plane_sum = plane_sum.at[:, target].add(jnp.stack([stream_part, span_part]))]
    mul x2 -> x0, other arithmetic: 14.1 us -> none  [the longest x1 8.77 us: derivatives(): (along_y[:, :, 2:, :] - along_y[:, :, :-2, :]) * metric[None, None, :, None]]
  transfers between devices with their start and end apart: 6 -> 0, of which waited for: 2 -> 0; matrix products, arithmetic and copies ran while one was open for 21% -> 0% of each run, Pallas kernels for 0% -> 0%
where the time goes in v1:
time: 60.9 us; the launch traced here: 60.7 us
  Pallas kernels  52.2 us (86%)
  local copies, waits for them, and re-layouts  7.8 us (13%)
  between operations  0.67 us (1%)
    pallas_call x1, Pallas kernels, per_device(): pl.pallas_call(kernel, name='substep', out_shape=jax.ShapeDtypeStruct(adj...  52.2 us
    unnamed x15, local copies, waits for them, and re-layouts  7.8 us

profile of v1, /device:TPU:1, one launch (start us, length us, event | category | flops | bytes accessed | tf_op | source)
XLA Modules:
  0.0 60.7 jit_solution(17924220677362712360)
XLA Ops:
  0.7 0.0 copy-start
  0.7 1.4 %copy-done = f32[3,16,64,128]{3,2,1,0:T(8,128)S(1)} copy-done((f32[3,16,64,128]{3,2,1,0:T(8,128)S(1)}, f32[3,16,64,128]{3,2,1,0:T(8,128)}, u32[]{:S(2)}) %copy-start) | copy-done | bytes 1572888
  2.1 0.0 copy-start.1
  2.1 1.4 %copy-done.1 = f32[3,16,64,128]{3,2,1,0:T(8,128)S(1)} copy-done((f32[3,16,64,128]{3,2,1,0:T(8,128)S(1)}, f32[3,16,64,128]{3,2,1,0:T(8,128)}, u32[]{:S(2)}) %copy-start.1) | copy-done | bytes 1572888
  3.5 0.0 copy-start.2
  3.5 1.2 %copy-done.2 = f32[512,512]{1,0:T(8,128)S(1)} copy-done((f32[512,512]{1,0:T(8,128)S(1)}, f32[512,512]{1,0:T(8,128)}, u32[]{:S(2)}) %copy-start.2) | copy-done | bytes 1048600
  4.7 0.0 copy-start.3
  4.7 0.7 %copy-done.3 = f32[64]{0:T(128)S(1)} copy-done((f32[64]{0:T(128)S(1)}, f32[64]{0:T(128)}, u32[]{:S(2)}) %copy-start.3) | copy-done | bytes 280
  5.4 0.0 copy-start.4
  5.4 0.7 %copy-done.4 = s32[128]{0:T(128)S(1)} copy-done((s32[128]{0:T(128)S(1)}, s32[128]{0:T(128)}, u32[]{:S(2)}) %copy-start.4) | copy-done | bytes 536
  6.0 0.0 copy-start.5
  6.0 0.7 %copy-done.5 = f32[128]{0:T(128)S(1)} copy-done((f32[128]{0:T(128)S(1)}, f32[128]{0:T(128)}, u32[]{:S(2)}) %copy-start.5) | copy-done | bytes 536
  6.7 0.0 copy-start.6
  6.7 0.7 %copy-done.6 = f32[128]{0:T(128)S(1)} copy-done((f32[128]{0:T(128)S(1)}, f32[128]{0:T(128)}, u32[]{:S(2)}) %copy-start.6) | copy-done | bytes 536
  7.3 52.2 %substep.1 = f32[3,16,64,128]{3,2,1,0:T(8,128)S(1)} custom-call(f32[48,64,128]{2,1,0:T(8,128)S(1)} %bitcast.6, f32[48,64,128]{2,1,0:T(8,128)S(1)} %bitcast.7, f32[1,64]{1,0:T(1,128)S(1)} %bitcast.8, f32[512,512]{1,0:T(8,128)S(1)} %copy-done.2, s32[1,128]{1,0:T(1,128)S(1)} %bitcast.9, f32[1,128]{1,0:T(1,128)S(1)} %bitcast.10, f32[1,128]{1,0:T(1,128)S(1)} %bitcast.11, ...), custom_call_target="tpu_custom_call" | custom-call | tf_op jit(solution)/shard_map/substep/pallas_call | solution.py:260
  59.6 1.1 %copy.11 = f32[3,16,64,128]{3,2,1,0:T(8,128)} copy(f32[3,16,64,128]{3,2,1,0:T(8,128)S(1)} %substep.1) | data formatting | bytes 3145728
Async XLA Ops:
  0.7 1.4 %copy-start = (f32[3,16,64,128]{3,2,1,0:T(8,128)S(1)}, f32[3,16,64,128]{3,2,1,0:T(8,128)}, u32[]{:S(2)}) copy-start(f32[3,16,64,128]{3,2,1,0:T(8,128)} %param.8) | copy-start | bytes 4718596
  2.1 1.4 %copy-start.1 = (f32[3,16,64,128]{3,2,1,0:T(8,128)S(1)}, f32[3,16,64,128]{3,2,1,0:T(8,128)}, u32[]{:S(2)}) copy-start(f32[3,16,64,128]{3,2,1,0:T(8,128)} %param.9) | copy-start | bytes 4718596
  3.5 1.2 %copy-start.2 = (f32[512,512]{1,0:T(8,128)S(1)}, f32[512,512]{1,0:T(8,128)}, u32[]{:S(2)}) copy-start(f32[512,512]{1,0:T(8,128)} %prop_ref.1) | copy-start | bytes 3145732
  4.7 0.7 %copy-start.3 = (f32[64]{0:T(128)S(1)}, f32[64]{0:T(128)}, u32[]{:S(2)}) copy-start(f32[64]{0:T(128)} %param.10) | copy-start | bytes 772
  5.4 0.7 %copy-start.4 = (s32[128]{0:T(128)S(1)}, s32[128]{0:T(128)}, u32[]{:S(2)}) copy-start(s32[128]{0:T(128)} %param.12) | copy-start | bytes 1540
  6.0 0.7 %copy-start.5 = (f32[128]{0:T(128)S(1)}, f32[128]{0:T(128)}, u32[]{:S(2)}) copy-start(f32[128]{0:T(128)} %param.13) | copy-start | bytes 1540
  6.7 0.7 %copy-start.6 = (f32[128]{0:T(128)S(1)}, f32[128]{0:T(128)}, u32[]{:S(2)}) copy-start(f32[128]{0:T(128)} %param.14) | copy-start | bytes 1540

commit v2 on v1

--- a/solution.py
+++ b/solution.py
@@ -18,6 +18,7 @@
 def kernel(
     adj_ref, base_ref, metric_ref, prop_ref, cell_ref, stream_ref, span_ref, count_ref,
     out_ref,
+    metric_in, cell_in, stream_in, span_in,
     fld, yh_out, yh_in, zh_out, zh_in, zh, met, send, cols, cols3, prop, prop3, rows_out,
     msg, slots, pick_rows, pick_cells, wall_part, wall_in,
     load_sem, y_send, y_recv, z_send, z_recv, f_send, f_recv, u_send, u_recv, own_sem,
@@ -41,6 +42,10 @@
         pltpu.make_async_copy(adj_ref, fld.at[pl.ds(0, 3 * planes), pl.ds(PAD, ny), :], load_sem.at[0]),
         pltpu.make_async_copy(base_ref, fld.at[pl.ds(3 * planes, 3 * planes), pl.ds(PAD, ny), :], load_sem.at[1]),
         pltpu.make_async_copy(prop_ref, prop, load_sem.at[2]),
+        pltpu.make_async_copy(metric_ref, metric_in, load_sem.at[3]),
+        pltpu.make_async_copy(cell_ref, cell_in, load_sem.at[4]),
+        pltpu.make_async_copy(stream_ref, stream_in, load_sem.at[5]),
+        pltpu.make_async_copy(span_ref, span_in, load_sem.at[6]),
     ]
     for load in loads:
         load.start()
@@ -51,18 +56,20 @@
     for o in range(1, SP):
         pl.semaphore_signal(barrier, inc=1, device_id=(w, (s + o) % SP), device_id_type=MESH)
 
+    for load in loads[3:]:
+        load.wait()
     alive = lax.broadcasted_iota(jnp.int32, (1, nz), 1) < count_ref[0]
     msg[...] = jnp.concatenate(
         [
-            cell_ref[...].astype(F32),
-            jnp.where(alive, stream_ref[...], 0.0),
-            jnp.where(alive, span_ref[...], 0.0),
+            cell_in[...].astype(F32),
+            jnp.where(alive, stream_in[...], 0.0),
+            jnp.where(alive, span_in[...], 0.0),
             jnp.zeros((5, nz), F32),
         ],
         0,
     )
     here = lax.broadcasted_iota(jnp.int32, (ny, ny), 0) == lax.broadcasted_iota(jnp.int32, (ny, ny), 1)
-    column = jnp.sum(jnp.where(here, jnp.broadcast_to(metric_ref[...], (ny, ny)), 0.0), 1, keepdims=True)
+    column = jnp.sum(jnp.where(here, jnp.broadcast_to(metric_in[...], (ny, ny)), 0.0), 1, keepdims=True)
     met[...] = jnp.broadcast_to(column, (ny, nz))
 
     loads[0].wait()
@@ -254,17 +261,19 @@
 ):
     comps, planes, ny, nz = adjoint.shape
     depth = propagator.shape[0]
-    vmem = pl.BlockSpec(memory_space=pltpu.VMEM)
-    anywhere = pl.BlockSpec(memory_space=pl.ANY)
+    hbm = pl.BlockSpec(memory_space=pltpu.HBM)
     dma = pltpu.SemaphoreType.DMA
     return pl.pallas_call(
         kernel,
         name="substep",
         out_shape=jax.ShapeDtypeStruct(adjoint.shape, F32),
-        in_specs=[anywhere, anywhere, vmem, anywhere, vmem, vmem, vmem,
-                  pl.BlockSpec(memory_space=pltpu.SMEM)],
-        out_specs=anywhere,
+        in_specs=[hbm] * 7 + [pl.BlockSpec(memory_space=pltpu.SMEM)],
+        out_specs=pl.BlockSpec(memory_space=pl.ANY),
         scratch_shapes=[
+            pltpu.VMEM((1, ny), F32),
+            pltpu.VMEM((1, nz), jnp.int32),
+            pltpu.VMEM((1, nz), F32),
+            pltpu.VMEM((1, nz), F32),
             pltpu.VMEM((NF * planes, ny + 2 * PAD, nz), F32),
             pltpu.VMEM((2, NF * planes, nz), F32),
             pltpu.VMEM((2, NF * planes, nz), F32),
@@ -284,7 +293,7 @@
             pltpu.VMEM((nz, SP * nz), BF16),
             pltpu.VMEM((4 * planes, nz), F32),
             pltpu.VMEM((WN, 8, nz), F32),
-            dma((3,)),
+            dma((7,)),
             dma((2,)), dma((2,)), dma((2,)), dma((2,)),
             dma((2, WN - 1)), dma((2, WN - 1)), dma((2, WN - 1)), dma((2, WN - 1)),
             dma((2,)),
@@ -293,13 +302,15 @@
         compiler_params=pltpu.CompilerParams(
             collective_id=0, has_side_effects=True, vmem_limit_bytes=48 << 20),
     )(
-        adjoint.reshape(comps * planes, ny, nz),
-        base_flow.reshape(comps * planes, ny, nz),
-        metric.reshape(1, ny),
-        propagator,
-        sensor_cell.reshape(1, nz),
-        stream_stress.reshape(1, nz),
-        span_stress.reshape(1, nz),
+        *(pltpu.with_memory_space_constraint(a, pltpu.HBM) for a in (
+            adjoint.reshape(comps * planes, ny, nz),
+            base_flow.reshape(comps * planes, ny, nz),
+            metric.reshape(1, ny),
+            propagator,
+            sensor_cell.reshape(1, nz),
+            stream_stress.reshape(1, nz),
+            span_stress.reshape(1, nz),
+        )),
         sensor_count,
     )
 

time: 60.9 us -> 54.5 us (0.89)
  local copies, waits for them, and re-layouts: 7.8 us -> 1.15 us
    unnamed x15 -> x1, local copies, waits for them, and re-layouts: 7.8 us -> 1.15 us
where the time goes in v2:
time: 54.5 us; the launch traced here: 54.4 us
  Pallas kernels  52.6 us (97%)
  local copies, waits for them, and re-layouts  1.15 us (2%)
  between operations  0.66 us (1%)
    pallas_call x1, Pallas kernels, per_device(): pl.pallas_call(kernel, name='substep', out_shape=jax.ShapeDtypeStruct(adj...  52.6 us
    unnamed x1, local copies, waits for them, and re-layouts  1.15 us

profile of v2, /device:TPU:1, one launch (start us, length us, event | category | flops | bytes accessed | tf_op | source)
XLA Modules:
  0.0 54.4 jit_solution(10431958357933173015)
XLA Ops:
  0.7 52.6 %substep.1 = f32[3,16,64,128]{3,2,1,0:T(8,128)S(1)} custom-call(f32[48,64,128]{2,1,0:T(8,128)} %bitcast.6, f32[48,64,128]{2,1,0:T(8,128)} %bitcast.7, f32[1,64]{1,0:T(1,128)} %bitcast.8, f32[512,512]{1,0:T(8,128)} %prop_ref.1, s32[1,128]{1,0:T(1,128)} %bitcast.9, f32[1,128]{1,0:T(1,128)} %bitcast.10, f32[1,128]{1,0:T(1,128)} %bitcast.11, s32[1]{0:T(128)S(6)} %copy.10.count_ref), custom_call_target="tpu_custom_call" | custom-call | tf_op jit(solution)/shard_map/substep/pallas_call | solution.py:266
  53.2 1.1 %copy.11 = f32[3,16,64,128]{3,2,1,0:T(8,128)} copy(f32[3,16,64,128]{3,2,1,0:T(8,128)S(1)} %substep.1) | data formatting | bytes 3145728

commit v3 on v2

v3 whole, which is shorter than its diff:
```python
import jax
import jax.numpy as jnp
from jax import lax
from jax.experimental import pallas as pl
from jax.experimental.pallas import tpu as pltpu
from jax.sharding import PartitionSpec as P

MESH = pl.DeviceIdType.MESH
BF16 = jnp.bfloat16
F32 = jnp.float32

NF = 6
PAD = 8
WN = 8
SP = 16


def kernel(
    adj_ref, base_ref, metric_ref, prop_ref, cell_ref, stream_ref, span_ref, count_ref,
    out_ref,
    metric_in, cell_in, stream_in, span_in,
    fld, yh_out, yh_in, zh_out, zh_in, fix, fix_out, fix_in, met,
    inner_out, edge_out, full_out, inner_in, edge_in, full_in, cols3, prop, prop3, rows_out,
    msg, slots, pick_rows, pick_cells, wall_part, wall_in,
    load_sem, y_send, y_recv, z_send, z_recv, x_send, x_recv, i_send, i_recv, e_send, e_recv,
    f_send, f_recv, u_send, u_recv, own_sem, s_send, s_recv, w_send, w_recv,
):
    planes = out_ref.shape[1]
    ny = out_ref.shape[2]
    nz = out_ref.shape[3]
    tall = ny + 2 * PAD
    blocks = ny // 8
    depth = prop.shape[1]
    w = lax.axis_index("wn")
    s = lax.axis_index("sp")
    lane = lax.broadcasted_iota(jnp.int32, (8, nz), 1)

    def peer(j):
        i = j // 2
        dy = (2 - i + 3 * (i // 2) - 2 * (i // 3)) % 4
        return ((w // 4 + 1 - j % 2) % 2) * 4 + (w + dy) % 4

    def to_peer(src, dst, send, recv, j):
        return pltpu.make_async_remote_copy(
            src, dst, send, recv, device_id=(peer(j), s), device_id_type=MESH)

    loads = [
        pltpu.make_async_copy(adj_ref, fld.at[pl.ds(0, 3 * planes), pl.ds(PAD, ny), :], load_sem.at[0]),
        pltpu.make_async_copy(base_ref, fld.at[pl.ds(3 * planes, 3 * planes), pl.ds(PAD, ny), :], load_sem.at[1]),
        pltpu.make_async_copy(prop_ref, prop, load_sem.at[2]),
        pltpu.make_async_copy(metric_ref, metric_in, load_sem.at[3]),
        pltpu.make_async_copy(cell_ref, cell_in, load_sem.at[4]),
        pltpu.make_async_copy(stream_ref, stream_in, load_sem.at[5]),
        pltpu.make_async_copy(span_ref, span_in, load_sem.at[6]),
    ]
    for at in (3, 4, 5, 6, 0, 1, 2):
        loads[at].start()

    barrier = pltpu.get_barrier_semaphore()
    for j in range(WN - 1):
        pl.semaphore_signal(barrier, inc=1, device_id=(peer(j), s), device_id_type=MESH)
    for o in range(1, SP):
        pl.semaphore_signal(barrier, inc=1, device_id=(w, (s + o) % SP), device_id_type=MESH)

    loads[3].wait()
    here = lax.broadcasted_iota(jnp.int32, (ny, ny), 0) == lax.broadcasted_iota(jnp.int32, (ny, ny), 1)
    column = jnp.sum(jnp.where(here, jnp.broadcast_to(metric_in[...], (ny, ny)), 0.0), 1, keepdims=True)
    met[...] = jnp.broadcast_to(2.0 * column, (ny, nz))

    for load in loads[4:]:
        load.wait()
    alive = lax.broadcasted_iota(jnp.int32, (1, nz), 1) < count_ref[0]
    msg[...] = jnp.concatenate(
        [
            cell_in[...].astype(F32),
            jnp.where(alive, stream_in[...], 0.0),
            jnp.where(alive, span_in[...], 0.0),
            jnp.zeros((5, nz), F32),
        ],
        0,
    )
    loads[0].wait()
    loads[1].wait()
    flat = fld.reshape(NF * planes * tall, nz)
    yh_out[0] = flat[pl.ds(PAD + ny - 1, NF * planes, stride=tall), :]
    yh_out[1] = flat[pl.ds(PAD, NF * planes, stride=tall), :]

    def forcing(x, at, rows, put):
        ahead, behind = (x + 1) % planes, (x + planes - 1) % planes
        m = met[pl.ds(at, rows), :]

        def read(f, plane, shift=0):
            return fld[f * planes + plane, pl.ds(PAD + shift + at, rows), :]

        mid = [read(f, x) for f in range(NF)]
        dx = [read(f, ahead) - read(f, behind) for f in range(NF)]
        dy = [read(f, x, 1) - read(f, x, -1) for f in range(NF)]
        dz = [pltpu.roll(mid[f], nz - 1, 1) - pltpu.roll(mid[f], 1, 1) for f in range(NF)]
        b1 = mid[4] * m
        for c in range(3):
            d = (dx, dy, dz)[c]
            stretch = mid[0] * d[3] + mid[1] * d[4] + mid[2] * d[5]
            if c == 1:
                stretch = stretch * m
            advect = mid[3] * dx[c] + b1 * dy[c] + mid[5] * dz[c]
            put(c, mid[c] + 0.125 * (advect - stretch))

    def fill(ref, x, first, rows):
        def put(c, value):
            ref[:, pl.ds(c * nz, nz)] = value

        forcing(x, first, rows, put)

    def fill_edges(ref, x):
        for at, to in ((0, 0), (ny - 8, 8)):
            def put(c, value, to=to):
                ref[pl.ds(to, 8), pl.ds(c * nz, nz)] = value

            forcing(x, at, 8, put)

    def inner_copy(j):
        return to_peer(inner_out.at[j], inner_in.at[w], i_send.at[j], i_recv.at[j], j)

    def edge_copy(j):
        return to_peer(edge_out.at[j], edge_in.at[w], e_send.at[j], e_recv.at[j], j)

    def full_copy(j):
        return to_peer(full_out.at[j], full_in.at[w], f_send.at[j], f_recv.at[j], j)

    def pack(r, carry):
        at = pl.multiple_of(r * 8, 8)
        for half in range(2):
            ends = jnp.zeros((8, nz), F32)
            for i in range(3 * planes):
                tile = fld[half * 3 * planes + i, pl.ds(PAD + at, 8), :]
                ends = jnp.where(lane // 2 == i, pltpu.roll(tile, 2 * i + 1, 1), ends)
            zh_out[half, pl.ds(at, 8), :] = ends
        return carry

    lax.fori_loop(0, blocks, pack, 0)
    fill(inner_out.at[0], 2 * peer(0), 8, ny - 16)
    pl.semaphore_wait(barrier, WN - 1 + SP - 1)
    y_halo, z_halo = [], []
    for side in range(2):
        step = 1 - 2 * side
        y_halo.append(pltpu.make_async_remote_copy(
            yh_out.at[side], yh_in.at[side], y_send.at[side], y_recv.at[side],
            device_id=((w + step) % WN, s), device_id_type=MESH))
        z_halo.append(pltpu.make_async_remote_copy(
            zh_out, zh_in.at[side], z_send.at[side], z_recv.at[side],
            device_id=(w, (s + step) % SP), device_id_type=MESH))
    for copy in y_halo:
        copy.start()
    for copy in z_halo:
        copy.start()
    inner_copy(0).start()

    slot_copies = [
        pltpu.make_async_remote_copy(
            msg, slots.at[o], s_send.at[o], s_recv.at[o],
            device_id=(w, (s + o) % SP), device_id_type=MESH)
        for o in range(1, SP)
    ]
    for copy in slot_copies:
        copy.start()
    slots[0] = msg[...]

    def inner(j, carry):
        fill(inner_out.at[j], 2 * peer(j), 8, ny - 16)
        inner_copy(j).start()
        return carry

    lax.fori_loop(1, WN - 1, inner, 0)
    fill(inner_in.at[w], 2 * w, 8, ny - 16)

    for copy in y_halo:
        copy.wait()
    flat[pl.ds(PAD - 1, NF * planes, stride=tall), :] = jnp.where(w == 0, 0.0, yh_in[0])
    flat[pl.ds(PAD + ny, NF * planes, stride=tall), :] = jnp.where(w == WN - 1, 0.0, yh_in[1])

    def edge(j, carry):
        fill_edges(edge_out.at[j], 2 * peer(j))
        edge_copy(j).start()
        return carry

    lax.fori_loop(0, WN - 1, edge, 0)
    fill_edges(edge_in.at[w], 2 * w)

    for copy in z_halo:
        copy.wait()
    group = lane // (2 * planes)
    packed = []
    for r in range(blocks):
        rows = pl.ds(8 * r, 8)
        own = [zh_out[half, rows, :] for half in range(2)]
        delta = [
            0.5 * jnp.where(
                lane % 2 == 0,
                pltpu.roll(zh_in[1, half, rows, :] - own[half], nz - 1, 1),
                pltpu.roll(own[half] - zh_in[0, half, rows, :], 1, 1))
            for half in range(2)
        ]
        b2 = jnp.where(
            group == 0, pltpu.roll(own[1], nz - 4 * planes, 1),
            jnp.where(group == 1, pltpu.roll(own[1], nz - 2 * planes, 1), own[1]))
        each = own[0] * delta[1]
        stretch = each + pltpu.roll(each, 2 * planes, 1) + pltpu.roll(each, 4 * planes, 1)
        packed.append(0.25 * (b2 * delta[0] - jnp.where(group == 2, stretch, 0.0)))
    for r in range(blocks):
        fix[r] = packed[r]

    def fix_of(to):
        out = jnp.zeros((8, nz), F32)
        for r in range(blocks):
            moved = pltpu.roll(fix[r], (nz + 4 * r - 4 * to) % nz, 1)
            out = jnp.where((lane % (2 * planes)) // 4 == r, moved, out)
        return out

    fix_copies = [to_peer(fix_out.at[j], fix_in.at[w], x_send.at[j], x_recv.at[j], j) for j in range(WN - 1)]
    for j in range(WN - 1):
        fix_out[j] = fix_of(peer(j))
        fix_copies[j].start()
    fix_in[w] = fix_of(w)

    for copy in slot_copies:
        copy.wait()
    n = 4 * planes
    for i in range(SP):
        got = slots[i]
        cell = got[0:1].astype(jnp.int32)
        side = cell // (planes * nz * SP)
        left = cell % (planes * nz * SP)
        key = (left // (nz * SP)) * 2 + side
        spot = left % (nz * SP) - s * nz
        row = lax.broadcasted_iota(jnp.int32, (n, nz), 0)
        parts = [got[1:2], got[2:3]]
        for p in range(3):
            tops = [v.astype(BF16).astype(F32) for v in parts]
            parts = [v - t for v, t in zip(parts, tops)]
            pick = jnp.where(row // 2 == key, jnp.where(row % 2 == 0, tops[0], tops[1]), 0.0)
            pick_rows[pl.ds(p * n, n), pl.ds(i * nz, nz)] = pick.astype(BF16)
        cells = lax.broadcasted_iota(jnp.int32, (nz, nz), 0)
        pick_cells[:, pl.ds(i * nz, nz)] = jnp.where(cells == spot, 1.0, 0.0).astype(BF16)
    summed = lax.dot_general(
        pick_rows[...], pick_cells[...], (((1,), (1,)), ((), ())), preferred_element_type=F32)
    wall_part[...] = summed[0:n] + summed[n:2 * n] + summed[2 * n:3 * n]
    wall_copies = [
        to_peer(wall_part.at[pl.ds(pl.multiple_of(peer(j) * 8, 8), 8), :], wall_in.at[j],
                w_send.at[j], w_recv.at[j], j)
        for j in range(WN - 1)
    ]
    for copy in wall_copies:
        copy.start()
    wall_in[WN - 1] = wall_part[pl.ds(pl.multiple_of(w * 8, 8), 8), :]

    def full(j, carry):
        fill(full_out.at[j], 2 * peer(j) + 1, 0, ny)
        full_copy(j).start()
        return carry

    lax.fori_loop(0, WN - 1, full, 0)
    fill(full_in.at[w], 2 * w + 1, 0, ny)

    loads[2].wait()
    whole = prop[...]
    high = whole.astype(BF16)
    prop3[:, pl.ds(0, depth)] = high
    prop3[:, pl.ds(depth, depth)] = (whole - high.astype(F32)).astype(BF16)
    prop3[:, pl.ds(2 * depth, depth)] = high

    def rows_copy(k, j):
        return to_peer(
            rows_out.at[k, :, pl.ds(pl.multiple_of(peer(j) * ny, ny), ny), :], out_ref.at[:, 2 * w + k],
            u_send.at[k, j], u_recv.at[k, j], j)

    own_copies = []
    for k in range(2):
        if k == 0:
            for j in range(WN - 1):
                inner_copy(j).wait_recv()
            for j in range(WN - 1):
                edge_copy(j).wait_recv()
            for copy in fix_copies + wall_copies:
                copy.wait()
            walls = wall_in[0]
            for j in range(1, WN):
                walls = walls + wall_in[j]
        else:
            for j in range(WN - 1):
                full_copy(j).wait_recv()
        ref, last = ((edge_in, 14), (full_in, ny - 2))[k]
        for side, (device, y) in enumerate(((0, 1), (WN - 1, last))):
            for comp, c in ((0, 0), (1, 2)):
                at = k * 4 + side * 2 + comp
                spot = (device, pl.ds(y, 1), pl.ds(c * nz, nz))
                ref[spot] = ref[spot] + walls[at:at + 1]

        def split(d, carry, k=k):
            if k == 0:
                ends = edge_in[d]
                whole = jnp.concatenate([ends[0:8], inner_in[d], ends[8:16]], 0)
            else:
                whole = full_in[d]
            change = fix_in[d]
            fixes = []
            for c in range(3):
                moved = [
                    pltpu.roll(change, (2 * nz - 1 - 2 * planes * c - 4 * r - 2 * k) % nz, 1)
                    for r in range(blocks)
                ]
                fixes.append(jnp.concatenate(
                    [jnp.where((lane == 0) | (lane == nz - 1), v, 0.0) for v in moved], 0))
            whole = whole + jnp.concatenate(fixes, 1)
            high = whole.astype(BF16)
            low = (whole - high.astype(F32)).astype(BF16)
            at = pl.multiple_of(d * ny, ny)
            cols3[pl.ds(at, ny), :] = high
            cols3[pl.ds(depth + at, ny), :] = high
            cols3[pl.ds(2 * depth + at, ny), :] = low
            return carry

        lax.fori_loop(0, WN, split, 0)
        updated = jnp.dot(prop3[...], cols3[...], preferred_element_type=F32)
        for c in range(3):
            rows_out[k, c] = updated[:, c * nz:(c + 1) * nz]
        for j in range(WN - 1):
            rows_copy(k, j).start()
        copy = pltpu.make_async_copy(
            rows_out.at[k, :, pl.ds(pl.multiple_of(w * ny, ny), ny), :], out_ref.at[:, 2 * w + k],
            own_sem.at[k])
        copy.start()
        own_copies.append(copy)
    for j in range(WN - 1):
        inner_copy(j).wait_send()
        edge_copy(j).wait_send()
        full_copy(j).wait_send()
    for k in range(2):
        for j in range(WN - 1):
            rows_copy(k, j).wait()
        own_copies[k].wait()


def per_device(
    adjoint, base_flow, metric, propagator, sensor_cell, stream_stress, span_stress, sensor_count
):
    comps, planes, ny, nz = adjoint.shape
    depth = propagator.shape[0]
    hbm = pl.BlockSpec(memory_space=pltpu.HBM)
    dma = pltpu.SemaphoreType.DMA
    return pl.pallas_call(
        kernel,
        name="substep",
        out_shape=jax.ShapeDtypeStruct(adjoint.shape, F32),
        in_specs=[hbm] * 7 + [pl.BlockSpec(memory_space=pltpu.SMEM)],
        out_specs=pl.BlockSpec(memory_space=pl.ANY),
        scratch_shapes=[
            pltpu.VMEM((1, ny), F32),
            pltpu.VMEM((1, nz), jnp.int32),
            pltpu.VMEM((1, nz), F32),
            pltpu.VMEM((1, nz), F32),
            pltpu.VMEM((NF * planes, ny + 2 * PAD, nz), F32),
            pltpu.VMEM((2, NF * planes, nz), F32),
            pltpu.VMEM((2, NF * planes, nz), F32),
            pltpu.VMEM((2, ny, nz), F32),
            pltpu.VMEM((2, 2, ny, nz), F32),
            pltpu.VMEM((ny // 8, 8, nz), F32),
            pltpu.VMEM((WN - 1, 8, nz), F32),
            pltpu.VMEM((WN, 8, nz), F32),
            pltpu.VMEM((ny, nz), F32),
            pltpu.VMEM((WN - 1, ny - 16, comps * nz), F32),
            pltpu.VMEM((WN - 1, 16, comps * nz), F32),
            pltpu.VMEM((WN - 1, ny, comps * nz), F32),
            pltpu.VMEM((WN, ny - 16, comps * nz), F32),
            pltpu.VMEM((WN, 16, comps * nz), F32),
            pltpu.VMEM((WN, ny, comps * nz), F32),
            pltpu.VMEM((3 * depth, comps * nz), BF16),
            pltpu.VMEM((depth, depth), F32),
            pltpu.VMEM((depth, 3 * depth), BF16),
            pltpu.VMEM((2, comps, depth, nz), F32),
            pltpu.VMEM((8, nz), F32),
            pltpu.VMEM((SP, 8, nz), F32),
            pltpu.VMEM((12 * planes, SP * nz), BF16),
            pltpu.VMEM((nz, SP * nz), BF16),
            pltpu.VMEM((4 * planes, nz), F32),
            pltpu.VMEM((WN, 8, nz), F32),
            dma((7,)),
            dma((2,)), dma((2,)), dma((2,)), dma((2,)),
            *([dma((WN - 1,))] * 8),
            dma((2, WN - 1)), dma((2, WN - 1)), dma((2,)),
            dma((SP,)), dma((SP,)), dma((WN - 1,)), dma((WN - 1,)),
        ],
        compiler_params=pltpu.CompilerParams(
            collective_id=0, has_side_effects=True, vmem_limit_bytes=48 << 20),
    )(
        *(pltpu.with_memory_space_constraint(a, pltpu.HBM) for a in (
            adjoint.reshape(comps * planes, ny, nz),
            base_flow.reshape(comps * planes, ny, nz),
            metric.reshape(1, ny),
            propagator,
            sensor_cell.reshape(1, nz),
            stream_stress.reshape(1, nz),
            span_stress.reshape(1, nz),
        )),
        sensor_count,
    )


def solution(mesh):
    placed = (
        P(None, None, "wn", "sp"),
        P(None, None, "wn", "sp"),
        P("wn"),
        P(),
        P(("wn", "sp")),
        P(("wn", "sp")),
        P(("wn", "sp")),
        P(("wn", "sp")),
    )
    return jax.shard_map(
        per_device, mesh=mesh, in_specs=placed, out_specs=P(None, None, "wn", "sp"), check_vma=False
    )
```

time: 54.5 us -> 51.4 us (0.943)
  Pallas kernels: 52.6 us -> 49.5 us
    pallas_call x1, Pallas kernels: 52.6 us -> 49.5 us  [per_device(): pl.pallas_call(kernel, name='substep', out_shape=jax.ShapeDtypeStruct(adj...]
where the time goes in v3:
time: 51.4 us; the launch traced here: 51.3 us
  Pallas kernels  49.5 us (96%)
  local copies, waits for them, and re-layouts  1.15 us (2%)
  between operations  0.66 us (1%)
    pallas_call x1, Pallas kernels, per_device(): pl.pallas_call(kernel, name='substep', out_shape=jax.ShapeDtypeStruct(adj...  49.5 us
    unnamed x1, local copies, waits for them, and re-layouts  1.15 us

profile of v3, /device:TPU:1, one launch (start us, length us, event | category | flops | bytes accessed | tf_op | source)
XLA Modules:
  0.0 51.3 jit_solution(16121068731526820304)
XLA Ops:
  0.7 49.5 %substep.1 = f32[3,16,64,128]{3,2,1,0:T(8,128)S(1)} custom-call(f32[48,64,128]{2,1,0:T(8,128)} %bitcast.6, f32[48,64,128]{2,1,0:T(8,128)} %bitcast.7, f32[1,64]{1,0:T(1,128)} %bitcast.8, f32[512,512]{1,0:T(8,128)} %prop_ref.1, s32[1,128]{1,0:T(1,128)} %bitcast.9, f32[1,128]{1,0:T(1,128)} %bitcast.10, f32[1,128]{1,0:T(1,128)} %bitcast.11, s32[1]{0:T(128)S(6)} %copy.10.count_ref), custom_call_target="tpu_custom_call" | custom-call | tf_op jit(solution)/shard_map/substep/pallas_call | solution.py:350
  50.2 1.1 %copy.11 = f32[3,16,64,128]{3,2,1,0:T(8,128)} copy(f32[3,16,64,128]{3,2,1,0:T(8,128)S(1)} %substep.1) | data formatting | bytes 3145728

commit v4 on v3

v4 whole, which is shorter than its diff:
```python
import jax
import jax.numpy as jnp
from jax import lax
from jax.experimental import pallas as pl
from jax.experimental.pallas import tpu as pltpu
from jax.sharding import PartitionSpec as P

MESH = pl.DeviceIdType.MESH
BF16 = jnp.bfloat16
F32 = jnp.float32

MSG = 4
NF = 6
PAD = 8
WN = 8
SP = 16
BLOCK = 8


def kernel(
    adj_ref, base_ref, metric_ref, prop_ref, cell_ref, stream_ref, span_ref, count_ref,
    out_ref,
    metric_in, cell_in, stream_in, span_in,
    fld, yh_out, yh_in, zh_out, zh_in, fix, fix_out, fix_in, met,
    inner_out, edge_out, full_out, inner_in, edge_in, full_in, cols3, prop, prop3, rows_out,
    msg, slots, pick_rows, pick_cells, wall_part, wall_in,
    load_sem, pair_sem, y_send, y_recv, z_send, z_recv, x_send, x_recv, i_send, i_recv, e_send, e_recv,
    f_send, f_recv, u_send, u_recv, own_sem, s_send, s_recv, w_send, w_recv,
):
    planes = out_ref.shape[1]
    ny = out_ref.shape[2]
    nz = out_ref.shape[3]
    tall = ny + 2 * PAD
    blocks = ny // 8
    depth = prop.shape[1]
    w = lax.axis_index("wn")
    s = lax.axis_index("sp")
    lane = lax.broadcasted_iota(jnp.int32, (8, nz), 1)

    def peer(j):
        i = j // 2
        dy = (2 - i + 3 * (i // 2) - 2 * (i // 3)) % 4
        return ((w // 4 + 1 - j % 2) % 2) * 4 + (w + dy) % 4

    def to_peer(src, dst, send, recv, j):
        return pltpu.make_async_remote_copy(
            src, dst, send, recv, device_id=(peer(j), s), device_id_type=MESH)

    barrier = pltpu.get_barrier_semaphore()
    row_peers = [(w, (s // BLOCK) * BLOCK + (s + o) % BLOCK) for o in range(1, BLOCK)]
    slot_peers = [((w + o) % WN, (s + (o // WN) * BLOCK) % SP) for o in range(1, 2 * WN)]
    greeted = row_peers + slot_peers + [(w, (s + 1) % SP), (w, (s + SP - 1) % SP)]

    small = [
        pltpu.make_async_copy(src, dst, load_sem.at[i])
        for i, (src, dst) in enumerate((
            (metric_ref, metric_in), (cell_ref, cell_in), (stream_ref, stream_in), (span_ref, span_in)))
    ]
    load_prop = pltpu.make_async_copy(prop_ref, prop, load_sem.at[4])
    fields = fld.reshape(NF, planes, tall, nz)
    flat = fld.reshape(NF * planes * tall, nz)
    pairs = planes // 2

    def load_pair(i):
        at = pl.multiple_of(2 * ((peer(0) + (pairs - i) % pairs) % pairs), 2)
        return [
            pltpu.make_async_copy(
                ref.at[:, pl.ds(at, 2)],
                fields.at[pl.ds(3 * half, 3), pl.ds(at, 2), pl.ds(PAD, ny), :],
                pair_sem.at[i, half])
            for half, ref in enumerate((adj_ref, base_ref))
        ]

    def wait_pairs(first, last):
        for i in range(first, last):
            for copy in load_pair(i):
                copy.wait()

    def forcing(x, at, rows, put):
        ahead, behind = (x + 1) % planes, (x + planes - 1) % planes
        m = met[pl.ds(at, rows), :]

        def read(f, plane, shift=0):
            return fld[f * planes + plane, pl.ds(PAD + shift + at, rows), :]

        mid = [read(f, x) for f in range(NF)]
        dx = [read(f, ahead) - read(f, behind) for f in range(NF)]
        dy = [read(f, x, 1) - read(f, x, -1) for f in range(NF)]
        dz = [pltpu.roll(mid[f], nz - 1, 1) - pltpu.roll(mid[f], 1, 1) for f in range(NF)]
        b1 = mid[4] * m
        for c in range(3):
            d = (dx, dy, dz)[c]
            stretch = mid[0] * d[3] + mid[1] * d[4] + mid[2] * d[5]
            if c == 1:
                stretch = stretch * m
            advect = mid[3] * dx[c] + b1 * dy[c] + mid[5] * dz[c]
            put(c, mid[c] + 0.125 * (advect - stretch))

    def fill(ref, x, first, rows):
        def put(c, value):
            ref[:, pl.ds(c * nz, nz)] = value

        forcing(x, first, rows, put)

    def fill_edges(ref, x):
        for at, to in ((0, 0), (ny - 8, 8)):
            def put(c, value, to=to):
                ref[pl.ds(to, 8), pl.ds(c * nz, nz)] = value

            forcing(x, at, 8, put)

    def inner_copy(j):
        return to_peer(inner_out.at[j], inner_in.at[w], i_send.at[j], i_recv.at[j], j)

    def edge_copy(j):
        return to_peer(edge_out.at[j], edge_in.at[w], e_send.at[j], e_recv.at[j], j)

    def full_copy(j):
        return to_peer(full_out.at[j], full_in.at[w], f_send.at[j], f_recv.at[j], j)

    y_halo, z_halo = [], []
    for side in range(2):
        step = 1 - 2 * side
        y_halo.append(pltpu.make_async_remote_copy(
            yh_out.at[side], yh_in.at[side], y_send.at[side], y_recv.at[side],
            device_id=((w + step) % WN, s), device_id_type=MESH))
        z_halo.append(pltpu.make_async_remote_copy(
            zh_out, zh_in.at[side], z_send.at[side], z_recv.at[side],
            device_id=(w, (s + step) % SP), device_id_type=MESH))
    slot_copies = [
        pltpu.make_async_remote_copy(
            msg, slots.at[o + 1], s_send.at[o], s_recv.at[o], device_id=device, device_id_type=MESH)
        for o, device in enumerate(slot_peers)
    ]
    fix_copies = [to_peer(fix_out.at[j], fix_in.at[w], x_send.at[j], x_recv.at[j], j) for j in range(WN - 1)]
    wall_copies = [
        pltpu.make_async_remote_copy(
            wall_part.at[pl.ds(pl.multiple_of(((s + o + 1) % BLOCK) * 8, 8), 8), :], wall_in.at[o + 1],
            w_send.at[o], w_recv.at[o], device_id=device, device_id_type=MESH)
        for o, device in enumerate(row_peers)
    ]

    def greet():
        for device in greeted:
            pl.semaphore_signal(barrier, inc=1, device_id=device, device_id_type=MESH)

    def start_loads():
        small[0].start()
        for i in range(pairs):
            for copy in load_pair(i):
                copy.start()
        for copy in small[1:] + [load_prop]:
            copy.start()

    def spread_metric():
        small[0].wait()
        here = lax.broadcasted_iota(jnp.int32, (ny, ny), 0) == lax.broadcasted_iota(jnp.int32, (ny, ny), 1)
        column = jnp.sum(jnp.where(here, jnp.broadcast_to(metric_in[...], (ny, ny)), 0.0), 1, keepdims=True)
        met[...] = jnp.broadcast_to(2.0 * column, (ny, nz))

    def send_slots():
        for copy in small[1:]:
            copy.wait()
        alive = lax.broadcasted_iota(jnp.int32, (1, nz), 1) < count_ref[0]
        msg[...] = jnp.concatenate(
            [
                cell_in[...].astype(F32),
                jnp.where(alive, stream_in[...], 0.0),
                jnp.where(alive, span_in[...], 0.0),
                jnp.zeros((MSG - 3, nz), F32),
            ],
            0,
        )
        for copy in slot_copies:
            copy.start()
        slots[0] = msg[...]

    def pack_y():
        yh_out[0] = flat[pl.ds(PAD + ny - 1, NF * planes, stride=tall), :]
        yh_out[1] = flat[pl.ds(PAD, NF * planes, stride=tall), :]

    def send_y():
        for copy in y_halo:
            copy.start()

    def pack_z():
        def pack(r, carry):
            at = pl.multiple_of(r * 8, 8)
            for half in range(2):
                ends = jnp.zeros((8, nz), F32)
                for i in range(3 * planes):
                    tile = fld[half * 3 * planes + i, pl.ds(PAD + at, 8), :]
                    ends = jnp.where(lane // 2 == i, pltpu.roll(tile, 2 * i + 1, 1), ends)
                zh_out[half, pl.ds(at, 8), :] = ends
            return carry

        lax.fori_loop(0, blocks, pack, 0)

    def send_z():
        for copy in z_halo:
            copy.start()

    def inner(j, carry=0):
        fill(inner_out.at[j], 2 * peer(j), 8, ny - 16)
        inner_copy(j).start()
        return carry

    def inners(first, last):
        lax.fori_loop(first, last, inner, 0)

    def inner_own():
        fill(inner_in.at[w], 2 * w, 8, ny - 16)

    def wait_y():
        for copy in y_halo:
            copy.wait()
        flat[pl.ds(PAD - 1, NF * planes, stride=tall), :] = jnp.where(w == 0, 0.0, yh_in[0])
        flat[pl.ds(PAD + ny, NF * planes, stride=tall), :] = jnp.where(w == WN - 1, 0.0, yh_in[1])

    def edge(j, carry):
        fill_edges(edge_out.at[j], 2 * peer(j))
        edge_copy(j).start()
        return carry

    def edges():
        lax.fori_loop(0, WN - 1, edge, 0)
        fill_edges(edge_in.at[w], 2 * w)

    def send_fix():
        for copy in z_halo:
            copy.wait()
        group = lane // (2 * planes)
        for r in range(blocks):
            rows = pl.ds(8 * r, 8)
            own = [zh_out[half, rows, :] for half in range(2)]
            delta = [
                0.5 * jnp.where(
                    lane % 2 == 0,
                    pltpu.roll(zh_in[1, half, rows, :] - own[half], nz - 1, 1),
                    pltpu.roll(own[half] - zh_in[0, half, rows, :], 1, 1))
                for half in range(2)
            ]
            b2 = jnp.where(
                group == 0, pltpu.roll(own[1], nz - 4 * planes, 1),
                jnp.where(group == 1, pltpu.roll(own[1], nz - 2 * planes, 1), own[1]))
            each = own[0] * delta[1]
            stretch = each + pltpu.roll(each, 2 * planes, 1) + pltpu.roll(each, 4 * planes, 1)
            fix[r] = 0.25 * (b2 * delta[0] - jnp.where(group == 2, stretch, 0.0))

        def fix_of(to):
            out = jnp.zeros((8, nz), F32)
            for r in range(blocks):
                moved = pltpu.roll(fix[r], (nz + 4 * r - 4 * to) % nz, 1)
                out = jnp.where((lane % (2 * planes)) // 4 == r, moved, out)
            return out

        for j in range(WN - 1):
            fix_out[j] = fix_of(peer(j))
            fix_copies[j].start()
        fix_in[w] = fix_of(w)

    def full(j, carry):
        fill(full_out.at[j], 2 * peer(j) + 1, 0, ny)
        full_copy(j).start()
        return carry

    def fulls(first, last):
        lax.fori_loop(first, last, full, 0)

    def full_own():
        fill(full_in.at[w], 2 * w + 1, 0, ny)

    def send_walls():
        for copy in slot_copies:
            copy.wait()
        n = 8 * BLOCK
        for i in range(2 * WN):
            got = slots[i]
            cell = got[0:1].astype(jnp.int32)
            side = cell // (planes * nz * SP)
            left = cell % (planes * nz * SP)
            plane, z = left // (nz * SP), left % (nz * SP)
            tile = z // nz
            ours = (plane // 2 == w) & (tile // BLOCK == s // BLOCK)
            key = jnp.where(ours, (tile % BLOCK) * 4 + (plane % 2) * 2 + side, -1)
            row = lax.broadcasted_iota(jnp.int32, (n, nz), 0)
            parts = [got[1:2], got[2:3]]
            for p in range(3):
                tops = [v.astype(BF16).astype(F32) for v in parts]
                parts = [v - t for v, t in zip(parts, tops)]
                pick = jnp.where(row // 2 == key, jnp.where(row % 2 == 0, tops[0], tops[1]), 0.0)
                pick_rows[pl.ds(p * n, n), pl.ds(i * nz, nz)] = pick.astype(BF16)
            cells = lax.broadcasted_iota(jnp.int32, (nz, nz), 0)
            pick_cells[:, pl.ds(i * nz, nz)] = jnp.where(cells == z % nz, 1.0, 0.0).astype(BF16)
        summed = lax.dot_general(
            pick_rows[...], pick_cells[...], (((1,), (1,)), ((), ())), preferred_element_type=F32)
        wall_part[...] = summed[0:n] + summed[n:2 * n] + summed[2 * n:3 * n]
        for copy in wall_copies:
            copy.start()
        wall_in[0] = wall_part[pl.ds(pl.multiple_of((s % BLOCK) * 8, 8), 8), :]

    def split_prop():
        load_prop.wait()
        whole = prop[...]
        high = whole.astype(BF16)
        prop3[:, pl.ds(0, depth)] = high
        prop3[:, pl.ds(depth, depth)] = (whole - high.astype(F32)).astype(BF16)
        prop3[:, pl.ds(2 * depth, depth)] = high

    def rows_copy(k, j):
        return to_peer(
            rows_out.at[k, :, pl.ds(pl.multiple_of(peer(j) * ny, ny), ny), :], out_ref.at[:, 2 * w + k],
            u_send.at[k, j], u_recv.at[k, j], j)

    greet()
    start_loads()
    spread_metric()
    wait_pairs(0, 2)
    fill(inner_out.at[0], 2*peer(0), 8, ny-16)
    pl.semaphore_wait(barrier,  len(greeted))
    inner_copy(0).start()
    send_slots()
    wait_pairs(2, pairs)
    pack_y()
    send_y()
    inners(1, WN-1)
    pack_z()
    send_z()
    inner_own()
    wait_y()
    edges()
    send_fix()
    send_walls()
    fulls(0, WN-1)
    full_own()
    split_prop()

    own_copies = []
    for k in range(2):
        if k == 0:
            for j in range(WN - 1):
                inner_copy(j).wait_recv()
            for j in range(WN - 1):
                edge_copy(j).wait_recv()
            for copy in fix_copies + wall_copies:
                copy.wait()
            walls = wall_in[0]
            for o in range(1, BLOCK):
                walls = walls + wall_in[o]
        else:
            for j in range(WN - 1):
                full_copy(j).wait_recv()
        ref, last = ((edge_in, 14), (full_in, ny - 2))[k]
        for side, (device, y) in enumerate(((0, 1), (WN - 1, last))):
            for comp, c in ((0, 0), (1, 2)):
                at = k * 4 + side * 2 + comp
                spot = (device, pl.ds(y, 1), pl.ds(c * nz, nz))
                ref[spot] = ref[spot] + walls[at:at + 1]

        def split(d, carry, k=k):
            if k == 0:
                ends = edge_in[d]
                whole = jnp.concatenate([ends[0:8], inner_in[d], ends[8:16]], 0)
            else:
                whole = full_in[d]
            change = fix_in[d]
            fixes = []
            for c in range(3):
                moved = [
                    pltpu.roll(change, (2 * nz - 1 - 2 * planes * c - 4 * r - 2 * k) % nz, 1)
                    for r in range(blocks)
                ]
                fixes.append(jnp.concatenate(
                    [jnp.where((lane == 0) | (lane == nz - 1), v, 0.0) for v in moved], 0))
            whole = whole + jnp.concatenate(fixes, 1)
            high = whole.astype(BF16)
            low = (whole - high.astype(F32)).astype(BF16)
            at = pl.multiple_of(d * ny, ny)
            cols3[pl.ds(at, ny), :] = high
            cols3[pl.ds(depth + at, ny), :] = high
            cols3[pl.ds(2 * depth + at, ny), :] = low
            return carry

        lax.fori_loop(0, WN, split, 0)
        updated = jnp.dot(prop3[...], cols3[...], preferred_element_type=F32)
        for c in range(3):
            rows_out[k, c] = updated[:, c * nz:(c + 1) * nz]
        for j in range(WN - 1):
            rows_copy(k, j).start()
        copy = pltpu.make_async_copy(
            rows_out.at[k, :, pl.ds(pl.multiple_of(w * ny, ny), ny), :], out_ref.at[:, 2 * w + k],
            own_sem.at[k])
        copy.start()
        own_copies.append(copy)
    for j in range(WN - 1):
        inner_copy(j).wait_send()
        edge_copy(j).wait_send()
        full_copy(j).wait_send()
    for k in range(2):
        for j in range(WN - 1):
            rows_copy(k, j).wait()
        own_copies[k].wait()


def per_device(
    adjoint, base_flow, metric, propagator, sensor_cell, stream_stress, span_stress, sensor_count
):
    comps, planes, ny, nz = adjoint.shape
    depth = propagator.shape[0]
    hbm = pl.BlockSpec(memory_space=pltpu.HBM)
    dma = pltpu.SemaphoreType.DMA
    return pl.pallas_call(
        kernel,
        name="substep",
        out_shape=jax.ShapeDtypeStruct(adjoint.shape, F32),
        in_specs=[hbm] * 7 + [pl.BlockSpec(memory_space=pltpu.SMEM)],
        out_specs=pl.BlockSpec(memory_space=pl.ANY),
        scratch_shapes=[
            pltpu.VMEM((1, ny), F32),
            pltpu.VMEM((1, nz), jnp.int32),
            pltpu.VMEM((1, nz), F32),
            pltpu.VMEM((1, nz), F32),
            pltpu.VMEM((NF * planes, ny + 2 * PAD, nz), F32),
            pltpu.VMEM((2, NF * planes, nz), F32),
            pltpu.VMEM((2, NF * planes, nz), F32),
            pltpu.VMEM((2, ny, nz), F32),
            pltpu.VMEM((2, 2, ny, nz), F32),
            pltpu.VMEM((ny // 8, 8, nz), F32),
            pltpu.VMEM((WN - 1, 8, nz), F32),
            pltpu.VMEM((WN, 8, nz), F32),
            pltpu.VMEM((ny, nz), F32),
            pltpu.VMEM((WN - 1, ny - 16, comps * nz), F32),
            pltpu.VMEM((WN - 1, 16, comps * nz), F32),
            pltpu.VMEM((WN - 1, ny, comps * nz), F32),
            pltpu.VMEM((WN, ny - 16, comps * nz), F32),
            pltpu.VMEM((WN, 16, comps * nz), F32),
            pltpu.VMEM((WN, ny, comps * nz), F32),
            pltpu.VMEM((3 * depth, comps * nz), BF16),
            pltpu.VMEM((depth, depth), F32),
            pltpu.VMEM((depth, 3 * depth), BF16),
            pltpu.VMEM((2, comps, depth, nz), F32),
            pltpu.VMEM((MSG, nz), F32),
            pltpu.VMEM((2 * WN, MSG, nz), F32),
            pltpu.VMEM((24 * BLOCK, 2 * WN * nz), BF16),
            pltpu.VMEM((nz, 2 * WN * nz), BF16),
            pltpu.VMEM((8 * BLOCK, nz), F32),
            pltpu.VMEM((BLOCK, 8, nz), F32),
            dma((5,)), dma((planes // 2, 2)),
            dma((2,)), dma((2,)), dma((2,)), dma((2,)),
            *([dma((WN - 1,))] * 8),
            dma((2, WN - 1)), dma((2, WN - 1)), dma((2,)),
            dma((2 * WN - 1,)), dma((2 * WN - 1,)), dma((BLOCK - 1,)), dma((BLOCK - 1,)),
        ],
        compiler_params=pltpu.CompilerParams(
            collective_id=0, has_side_effects=True, vmem_limit_bytes=48 << 20),
    )(
        *(pltpu.with_memory_space_constraint(a, pltpu.HBM) for a in (
            adjoint,
            base_flow,
            metric.reshape(1, ny),
            propagator,
            sensor_cell.reshape(1, nz),
            stream_stress.reshape(1, nz),
            span_stress.reshape(1, nz),
        )),
        sensor_count,
    )


def solution(mesh):
    placed = (
        P(None, None, "wn", "sp"),
        P(None, None, "wn", "sp"),
        P("wn"),
        P(),
        P(("wn", "sp")),
        P(("wn", "sp")),
        P(("wn", "sp")),
        P(("wn", "sp")),
    )
    return jax.shard_map(
        per_device, mesh=mesh, in_specs=placed, out_specs=P(None, None, "wn", "sp"), check_vma=False
    )
```

time: 51.4 us -> 50.2 us (0.977)
  Pallas kernels: 49.5 us -> 48.3 us
    pallas_call x1, Pallas kernels: 49.5 us -> 48.3 us  [per_device(): pl.pallas_call(kernel, name='substep', out_shape=jax.ShapeDtypeStruct(adj...]
where the time goes in v4:
time: 50.2 us; the launch traced here: 50.1 us
  Pallas kernels  48.3 us (96%)
  local copies, waits for them, and re-layouts  1.15 us (2%)
  between operations  0.66 us (1%)
    pallas_call x1, Pallas kernels, per_device(): pl.pallas_call(kernel, name='substep', out_shape=jax.ShapeDtypeStruct(adj...  48.3 us
    unnamed x1, local copies, waits for them, and re-layouts  1.15 us

profile of v4, /device:TPU:1, one launch (start us, length us, event | category | flops | bytes accessed | tf_op | source)
XLA Modules:
  0.0 50.1 jit_solution(318590061945548805)
XLA Ops:
  0.7 48.3 %substep.1 = f32[3,16,64,128]{3,2,1,0:T(8,128)S(1)} custom-call(f32[3,16,64,128]{3,2,1,0:T(8,128)} %adj_ref.1, f32[3,16,64,128]{3,2,1,0:T(8,128)} %base_ref.1, f32[1,64]{1,0:T(1,128)} %bitcast.4, f32[512,512]{1,0:T(8,128)} %prop_ref.1, s32[1,128]{1,0:T(1,128)} %bitcast.5, f32[1,128]{1,0:T(1,128)} %bitcast.6, f32[1,128]{1,0:T(1,128)} %bitcast.7, ...), custom_call_target="tpu_custom_call" | custom-call | tf_op jit(solution)/shard_map/substep/pallas_call | solution.py:412
  49.0 1.1 %copy.11 = f32[3,16,64,128]{3,2,1,0:T(8,128)} copy(f32[3,16,64,128]{3,2,1,0:T(8,128)S(1)} %substep.1) | data formatting | bytes 3145728

commit v5 on v4

--- a/solution.py
+++ b/solution.py
@@ -9,7 +9,7 @@
 BF16 = jnp.bfloat16
 F32 = jnp.float32
 
-MSG = 4
+MSG = 3
 NF = 6
 PAD = 8
 WN = 8
@@ -21,11 +21,11 @@
     adj_ref, base_ref, metric_ref, prop_ref, cell_ref, stream_ref, span_ref, count_ref,
     out_ref,
     metric_in, cell_in, stream_in, span_in,
-    fld, yh_out, yh_in, zh_out, zh_in, fix, fix_out, fix_in, met,
-    inner_out, edge_out, full_out, inner_in, edge_in, full_in, cols3, prop, prop3, rows_out,
+    fld, yh_out, yh_in, ends_own, zh_out, zh_in, fix, fix_out, fix_in, met,
+    inner_out, edge_out, inner_in, edge_in, cols3, prop, prop3, rows_out,
     msg, slots, pick_rows, pick_cells, wall_part, wall_in,
     load_sem, pair_sem, y_send, y_recv, z_send, z_recv, x_send, x_recv, i_send, i_recv, e_send, e_recv,
-    f_send, f_recv, u_send, u_recv, own_sem, s_send, s_recv, w_send, w_recv,
+    u_send, u_recv, own_sem, s_send, s_recv, w_send, w_recv,
 ):
     planes = out_ref.shape[1]
     ny = out_ref.shape[2]
@@ -109,14 +109,11 @@
 
             forcing(x, at, 8, put)
 
-    def inner_copy(j):
-        return to_peer(inner_out.at[j], inner_in.at[w], i_send.at[j], i_recv.at[j], j)
-
-    def edge_copy(j):
-        return to_peer(edge_out.at[j], edge_in.at[w], e_send.at[j], e_recv.at[j], j)
-
-    def full_copy(j):
-        return to_peer(full_out.at[j], full_in.at[w], f_send.at[j], f_recv.at[j], j)
+    def inner_copy(k, j):
+        return to_peer(inner_out.at[k, j], inner_in.at[k, w], i_send.at[k, j], i_recv.at[k, j], j)
+
+    def edge_copy(k, j):
+        return to_peer(edge_out.at[k, j], edge_in.at[k, w], e_send.at[k, j], e_recv.at[k, j], j)
 
     y_halo, z_halo = [], []
     for side in range(2):
@@ -125,7 +122,7 @@
             yh_out.at[side], yh_in.at[side], y_send.at[side], y_recv.at[side],
             device_id=((w + step) % WN, s), device_id_type=MESH))
         z_halo.append(pltpu.make_async_remote_copy(
-            zh_out, zh_in.at[side], z_send.at[side], z_recv.at[side],
+            zh_out.at[side], zh_in.at[side], z_send.at[side], z_recv.at[side],
             device_id=(w, (s + step) % SP), device_id_type=MESH))
     slot_copies = [
         pltpu.make_async_remote_copy(
@@ -158,7 +155,7 @@
         column = jnp.sum(jnp.where(here, jnp.broadcast_to(metric_in[...], (ny, ny)), 0.0), 1, keepdims=True)
         met[...] = jnp.broadcast_to(2.0 * column, (ny, nz))
 
-    def send_slots():
+    def build_slots():
         for copy in small[1:]:
             copy.wait()
         alive = lax.broadcasted_iota(jnp.int32, (1, nz), 1) < count_ref[0]
@@ -167,31 +164,37 @@
                 cell_in[...].astype(F32),
                 jnp.where(alive, stream_in[...], 0.0),
                 jnp.where(alive, span_in[...], 0.0),
-                jnp.zeros((MSG - 3, nz), F32),
             ],
             0,
         )
+        slots[0] = msg[...]
+
+    def start_slots():
         for copy in slot_copies:
             copy.start()
-        slots[0] = msg[...]
 
     def pack_y():
         yh_out[0] = flat[pl.ds(PAD + ny - 1, NF * planes, stride=tall), :]
         yh_out[1] = flat[pl.ds(PAD, NF * planes, stride=tall), :]
 
     def send_y():
-        for copy in y_halo:
-            copy.start()
+        pl.when(w != WN - 1)(y_halo[0].start)
+        pl.when(w != 0)(y_halo[1].start)
 
     def pack_z():
         def pack(r, carry):
             at = pl.multiple_of(r * 8, 8)
+            halves = []
             for half in range(2):
                 ends = jnp.zeros((8, nz), F32)
                 for i in range(3 * planes):
                     tile = fld[half * 3 * planes + i, pl.ds(PAD + at, 8), :]
                     ends = jnp.where(lane // 2 == i, pltpu.roll(tile, 2 * i + 1, 1), ends)
-                zh_out[half, pl.ds(at, 8), :] = ends
+                ends_own[half, pl.ds(at, 8), :] = ends
+                halves.append(ends)
+            even = lane % 2 == 0
+            zh_out[0, pl.ds(at, 8), :] = jnp.where(even, halves[0], pltpu.roll(halves[1], 1, 1))
+            zh_out[1, pl.ds(at, 8), :] = jnp.where(even, pltpu.roll(halves[1], nz - 1, 1), halves[0])
             return carry
 
         lax.fori_loop(0, blocks, pack, 0)
@@ -200,31 +203,44 @@
         for copy in z_halo:
             copy.start()
 
-    def inner(j, carry=0):
-        fill(inner_out.at[j], 2 * peer(j), 8, ny - 16)
-        inner_copy(j).start()
-        return carry
-
-    def inners(first, last):
+    def fill_inner(k, j):
+        fill(inner_out.at[k, j], 2 * peer(j) + k, 8, ny - 16)
+
+    def inners(k, first, last):
+        def inner(j, carry):
+            fill_inner(k, j)
+            inner_copy(k, j).start()
+            return carry
+
         lax.fori_loop(first, last, inner, 0)
 
-    def inner_own():
-        fill(inner_in.at[w], 2 * w, 8, ny - 16)
+    def inner_own(k):
+        fill(inner_in.at[k, w], 2 * w + k, 8, ny - 16)
 
     def wait_y():
-        for copy in y_halo:
-            copy.wait()
-        flat[pl.ds(PAD - 1, NF * planes, stride=tall), :] = jnp.where(w == 0, 0.0, yh_in[0])
-        flat[pl.ds(PAD + ny, NF * planes, stride=tall), :] = jnp.where(w == WN - 1, 0.0, yh_in[1])
-
-    def edge(j, carry):
-        fill_edges(edge_out.at[j], 2 * peer(j))
-        edge_copy(j).start()
-        return carry
-
-    def edges():
+        for side, (edge_of_wall, row) in enumerate(((0, PAD - 1), (WN - 1, PAD + ny))):
+            spot = (pl.ds(row, NF * planes, stride=tall), slice(None))
+
+            @pl.when(w != edge_of_wall)
+            def _(side=side, spot=spot):
+                y_halo[side].wait_recv()
+                flat[spot] = yh_in[side]
+
+            @pl.when(w == edge_of_wall)
+            def _(spot=spot):
+                flat[spot] = jnp.zeros((NF * planes, nz), F32)
+
+        pl.when(w != WN - 1)(y_halo[0].wait_send)
+        pl.when(w != 0)(y_halo[1].wait_send)
+
+    def edges(k):
+        def edge(j, carry):
+            fill_edges(edge_out.at[k, j], 2 * peer(j) + k)
+            edge_copy(k, j).start()
+            return carry
+
         lax.fori_loop(0, WN - 1, edge, 0)
-        fill_edges(edge_in.at[w], 2 * w)
+        fill_edges(edge_in.at[k, w], 2 * w + k)
 
     def send_fix():
         for copy in z_halo:
@@ -232,12 +248,15 @@
         group = lane // (2 * planes)
         for r in range(blocks):
             rows = pl.ds(8 * r, 8)
-            own = [zh_out[half, rows, :] for half in range(2)]
+            own = [ends_own[half, rows, :] for half in range(2)]
+            before, after = zh_in[0, rows, :], zh_in[1, rows, :]
+            before = [before, pltpu.roll(before, nz - 1, 1)]
+            after = [after, pltpu.roll(after, 1, 1)]
             delta = [
                 0.5 * jnp.where(
                     lane % 2 == 0,
-                    pltpu.roll(zh_in[1, half, rows, :] - own[half], nz - 1, 1),
-                    pltpu.roll(own[half] - zh_in[0, half, rows, :], 1, 1))
+                    pltpu.roll(after[half] - own[half], nz - 1, 1),
+                    pltpu.roll(own[half] - before[half], 1, 1))
                 for half in range(2)
             ]
             b2 = jnp.where(
@@ -258,17 +277,6 @@
             fix_out[j] = fix_of(peer(j))
             fix_copies[j].start()
         fix_in[w] = fix_of(w)
-
-    def full(j, carry):
-        fill(full_out.at[j], 2 * peer(j) + 1, 0, ny)
-        full_copy(j).start()
-        return carry
-
-    def fulls(first, last):
-        lax.fori_loop(first, last, full, 0)
-
-    def full_own():
-        fill(full_in.at[w], 2 * w + 1, 0, ny)
 
     def send_walls():
         for copy in slot_copies:
@@ -315,54 +323,50 @@
     greet()
     start_loads()
     spread_metric()
-    wait_pairs(0, 2)
-    fill(inner_out.at[0], 2*peer(0), 8, ny-16)
-    pl.semaphore_wait(barrier,  len(greeted))
-    inner_copy(0).start()
-    send_slots()
-    wait_pairs(2, pairs)
+    wait_pairs(0, pairs)
     pack_y()
+    fill_inner(0, 0)
+    fill_inner(0, 1)
+    build_slots()
+    pl.semaphore_wait(barrier, len(greeted))
+    inner_copy(0, 0).start()
+    inner_copy(0, 1).start()
     send_y()
-    inners(1, WN-1)
+    start_slots()
+    inners(0, 2, WN - 1)
     pack_z()
     send_z()
-    inner_own()
+    inner_own(0)
+    inners(1, 0, 2)
     wait_y()
-    edges()
+    edges(0)
     send_fix()
     send_walls()
-    fulls(0, WN-1)
-    full_own()
+    inners(1, 2, WN - 1)
+    edges(1)
+    inner_own(1)
     split_prop()
 
     own_copies = []
     for k in range(2):
+        for j in range(WN - 1):
+            inner_copy(k, j).wait_recv()
+            edge_copy(k, j).wait_recv()
         if k == 0:
-            for j in range(WN - 1):
-                inner_copy(j).wait_recv()
-            for j in range(WN - 1):
-                edge_copy(j).wait_recv()
             for copy in fix_copies + wall_copies:
                 copy.wait()
             walls = wall_in[0]
             for o in range(1, BLOCK):
                 walls = walls + wall_in[o]
-        else:
-            for j in range(WN - 1):
-                full_copy(j).wait_recv()
-        ref, last = ((edge_in, 14), (full_in, ny - 2))[k]
-        for side, (device, y) in enumerate(((0, 1), (WN - 1, last))):
+        for side, (device, y) in enumerate(((0, 1), (WN - 1, 14))):
             for comp, c in ((0, 0), (1, 2)):
                 at = k * 4 + side * 2 + comp
-                spot = (device, pl.ds(y, 1), pl.ds(c * nz, nz))
-                ref[spot] = ref[spot] + walls[at:at + 1]
+                spot = (k, device, pl.ds(y, 1), pl.ds(c * nz, nz))
+                edge_in[spot] = edge_in[spot] + walls[at:at + 1]
 
         def split(d, carry, k=k):
-            if k == 0:
-                ends = edge_in[d]
-                whole = jnp.concatenate([ends[0:8], inner_in[d], ends[8:16]], 0)
-            else:
-                whole = full_in[d]
+            ends = edge_in[k, d]
+            whole = jnp.concatenate([ends[0:8], inner_in[k, d], ends[8:16]], 0)
             change = fix_in[d]
             fixes = []
             for c in range(3):
@@ -392,10 +396,10 @@
             own_sem.at[k])
         copy.start()
         own_copies.append(copy)
-    for j in range(WN - 1):
-        inner_copy(j).wait_send()
-        edge_copy(j).wait_send()
-        full_copy(j).wait_send()
+    for k in range(2):
+        for j in range(WN - 1):
+            inner_copy(k, j).wait_send()
+            edge_copy(k, j).wait_send()
     for k in range(2):
         for j in range(WN - 1):
             rows_copy(k, j).wait()
@@ -424,17 +428,16 @@
             pltpu.VMEM((2, NF * planes, nz), F32),
             pltpu.VMEM((2, NF * planes, nz), F32),
             pltpu.VMEM((2, ny, nz), F32),
-            pltpu.VMEM((2, 2, ny, nz), F32),
+            pltpu.VMEM((2, ny, nz), F32),
+            pltpu.VMEM((2, ny, nz), F32),
             pltpu.VMEM((ny // 8, 8, nz), F32),
             pltpu.VMEM((WN - 1, 8, nz), F32),
             pltpu.VMEM((WN, 8, nz), F32),
             pltpu.VMEM((ny, nz), F32),
-            pltpu.VMEM((WN - 1, ny - 16, comps * nz), F32),
-            pltpu.VMEM((WN - 1, 16, comps * nz), F32),
-            pltpu.VMEM((WN - 1, ny, comps * nz), F32),
-            pltpu.VMEM((WN, ny - 16, comps * nz), F32),
-            pltpu.VMEM((WN, 16, comps * nz), F32),
-            pltpu.VMEM((WN, ny, comps * nz), F32),
+            pltpu.VMEM((2, WN - 1, ny - 16, comps * nz), F32),
+            pltpu.VMEM((2, WN - 1, 16, comps * nz), F32),
+            pltpu.VMEM((2, WN, ny - 16, comps * nz), F32),
+            pltpu.VMEM((2, WN, 16, comps * nz), F32),
             pltpu.VMEM((3 * depth, comps * nz), BF16),
             pltpu.VMEM((depth, depth), F32),
             pltpu.VMEM((depth, 3 * depth), BF16),
@@ -447,8 +450,8 @@
             pltpu.VMEM((BLOCK, 8, nz), F32),
             dma((5,)), dma((planes // 2, 2)),
             dma((2,)), dma((2,)), dma((2,)), dma((2,)),
-            *([dma((WN - 1,))] * 8),
-            dma((2, WN - 1)), dma((2, WN - 1)), dma((2,)),
+            dma((WN - 1,)), dma((WN - 1,)),
+            *([dma((2, WN - 1))] * 6), dma((2,)),
             dma((2 * WN - 1,)), dma((2 * WN - 1,)), dma((BLOCK - 1,)), dma((BLOCK - 1,)),
         ],
         compiler_params=pltpu.CompilerParams(

time: 50.2 us -> 48.9 us (0.974)
  Pallas kernels: 48.3 us -> 47 us
    pallas_call x1, Pallas kernels: 48.3 us -> 47 us  [per_device(): pl.pallas_call(kernel, name='substep', out_shape=jax.ShapeDtypeStruct(adj...]
where the time goes in v5:
time: 48.9 us; the launch traced here: 48.8 us
  Pallas kernels  47 us (96%)
  local copies, waits for them, and re-layouts  1.15 us (2%)
  between operations  0.66 us (1%)
    pallas_call x1, Pallas kernels, per_device(): pl.pallas_call(kernel, name='substep', out_shape=jax.ShapeDtypeStruct(adj...  47 us
    unnamed x1, local copies, waits for them, and re-layouts  1.15 us

profile of v5, /device:TPU:1, one launch (start us, length us, event | category | flops | bytes accessed | tf_op | source)
XLA Modules:
  0.0 48.8 jit_solution(5560434882640458791)
XLA Ops:
  0.7 47.0 %substep.1 = f32[3,16,64,128]{3,2,1,0:T(8,128)S(1)} custom-call(f32[3,16,64,128]{3,2,1,0:T(8,128)} %adj_ref.1, f32[3,16,64,128]{3,2,1,0:T(8,128)} %base_ref.1, f32[1,64]{1,0:T(1,128)} %bitcast.4, f32[512,512]{1,0:T(8,128)} %prop_ref.1, s32[1,128]{1,0:T(1,128)} %bitcast.5, f32[1,128]{1,0:T(1,128)} %bitcast.6, f32[1,128]{1,0:T(1,128)} %bitcast.7, ...), custom_call_target="tpu_custom_call" | custom-call | tf_op jit(solution)/shard_map/substep/pallas_call | solution.py:416
  47.7 1.1 %copy.11 = f32[3,16,64,128]{3,2,1,0:T(8,128)} copy(f32[3,16,64,128]{3,2,1,0:T(8,128)S(1)} %substep.1) | data formatting | bytes 3145728

commit v6 on v5

--- a/solution.py
+++ b/solution.py
@@ -9,7 +9,7 @@
 BF16 = jnp.bfloat16
 F32 = jnp.float32
 
-MSG = 3
+MSG = 8
 NF = 6
 PAD = 8
 WN = 8
@@ -36,20 +36,31 @@
     w = lax.axis_index("wn")
     s = lax.axis_index("sp")
     lane = lax.broadcasted_iota(jnp.int32, (8, nz), 1)
+    row8 = lax.broadcasted_iota(jnp.int32, (8, nz), 0)
+
+    mirror = 1 - 2 * lax.rem(s, 2)
+    half, along = lax.div(w, 4), lax.rem(w, 4) + 4
+    steps = ((2, 1), (1, 1), (-1, 0), (0, 1), (-1, 1), (1, 0), (2, 0), (0, 0))
 
     def peer(j):
-        i = j // 2
-        dy = (2 - i + 3 * (i // 2) - 2 * (i // 3)) % 4
-        return ((w // 4 + 1 - j % 2) % 2) * 4 + (w + dy) % 4
+        if isinstance(j, int):
+            dy, dz = steps[j]
+        else:
+            dy, dz = 0, 0
+            for i, (y, z) in enumerate(steps):
+                dy, dz = jnp.where(j == i, y, dy), jnp.where(j == i, z, dz)
+        return lax.rem(half + dz, 2) * 4 + lax.rem(along + dy * mirror, 4)
 
     def to_peer(src, dst, send, recv, j):
         return pltpu.make_async_remote_copy(
             src, dst, send, recv, device_id=(peer(j), s), device_id_type=MESH)
 
     barrier = pltpu.get_barrier_semaphore()
-    row_peers = [(w, (s // BLOCK) * BLOCK + (s + o) % BLOCK) for o in range(1, BLOCK)]
-    slot_peers = [((w + o) % WN, (s + (o // WN) * BLOCK) % SP) for o in range(1, 2 * WN)]
-    greeted = row_peers + slot_peers + [(w, (s + 1) % SP), (w, (s + SP - 1) % SP)]
+    base = s - lax.rem(s, BLOCK)
+    row_peers = [(w, base + lax.rem(s + o, BLOCK)) for o in range(1, BLOCK)]
+    across = lax.rem(s + BLOCK, SP)
+    slot_peers = [(lax.rem(w + o, WN), across if o >= WN else s) for o in range(1, 2 * WN)]
+    greeted = row_peers + slot_peers + [(w, lax.rem(s + 1, SP)), (w, lax.rem(s + SP - 1, SP))]
 
     small = [
         pltpu.make_async_copy(src, dst, load_sem.at[i])
@@ -62,7 +73,7 @@
     pairs = planes // 2
 
     def load_pair(i):
-        at = pl.multiple_of(2 * ((peer(0) + (pairs - i) % pairs) % pairs), 2)
+        at = pl.multiple_of(2 * lax.rem(peer(0) + (pairs - i) % pairs, pairs), 2)
         return [
             pltpu.make_async_copy(
                 ref.at[:, pl.ds(at, 2)],
@@ -77,7 +88,7 @@
                 copy.wait()
 
     def forcing(x, at, rows, put):
-        ahead, behind = (x + 1) % planes, (x + planes - 1) % planes
+        ahead, behind = lax.rem(x + 1, planes), lax.rem(x + planes - 1, planes)
         m = met[pl.ds(at, rows), :]
 
         def read(f, plane, shift=0):
@@ -120,10 +131,10 @@
         step = 1 - 2 * side
         y_halo.append(pltpu.make_async_remote_copy(
             yh_out.at[side], yh_in.at[side], y_send.at[side], y_recv.at[side],
-            device_id=((w + step) % WN, s), device_id_type=MESH))
+            device_id=(lax.rem(w + WN + step, WN), s), device_id_type=MESH))
         z_halo.append(pltpu.make_async_remote_copy(
             zh_out.at[side], zh_in.at[side], z_send.at[side], z_recv.at[side],
-            device_id=(w, (s + step) % SP), device_id_type=MESH))
+            device_id=(w, lax.rem(s + SP + step, SP)), device_id_type=MESH))
     slot_copies = [
         pltpu.make_async_remote_copy(
             msg, slots.at[o + 1], s_send.at[o], s_recv.at[o], device_id=device, device_id_type=MESH)
@@ -164,6 +175,7 @@
                 cell_in[...].astype(F32),
                 jnp.where(alive, stream_in[...], 0.0),
                 jnp.where(alive, span_in[...], 0.0),
+                jnp.zeros((MSG - 3, nz), F32),
             ],
             0,
         )
@@ -358,11 +370,11 @@
             walls = wall_in[0]
             for o in range(1, BLOCK):
                 walls = walls + wall_in[o]
-        for side, (device, y) in enumerate(((0, 1), (WN - 1, 14))):
+        for side, (device, y) in enumerate(((0, 1), (WN - 1, 6))):
             for comp, c in ((0, 0), (1, 2)):
                 at = k * 4 + side * 2 + comp
-                spot = (k, device, pl.ds(y, 1), pl.ds(c * nz, nz))
-                edge_in[spot] = edge_in[spot] + walls[at:at + 1]
+                spot = (k, device, pl.ds(8 * side, 8), pl.ds(c * nz, nz))
+                edge_in[spot] = edge_in[spot] + jnp.where(row8 == y, walls[at:at + 1], 0.0)
 
         def split(d, carry, k=k):
             ends = edge_in[k, d]

time: 48.9 us -> 49.1 us (level)
  no operation moved by 1% of the time
where the time goes in v6:
time: 49.1 us; the launch traced here: 49 us
  Pallas kernels  47.2 us (96%)
  local copies, waits for them, and re-layouts  1.15 us (2%)
  between operations  0.66 us (1%)
    pallas_call x1, Pallas kernels, per_device(): pl.pallas_call(kernel, name='substep', out_shape=jax.ShapeDtypeStruct(adj...  47.2 us
    unnamed x1, local copies, waits for them, and re-layouts  1.15 us

profile of v6, /device:TPU:1, one launch (start us, length us, event | category | flops | bytes accessed | tf_op | source)
XLA Modules:
  0.0 49.0 jit_solution(16000213436871443187)
XLA Ops:
  0.7 47.2 %substep.1 = f32[3,16,64,128]{3,2,1,0:T(8,128)S(1)} custom-call(f32[3,16,64,128]{3,2,1,0:T(8,128)} %adj_ref.1, f32[3,16,64,128]{3,2,1,0:T(8,128)} %base_ref.1, f32[1,64]{1,0:T(1,128)} %bitcast.4, f32[512,512]{1,0:T(8,128)} %prop_ref.1, s32[1,128]{1,0:T(1,128)} %bitcast.5, f32[1,128]{1,0:T(1,128)} %bitcast.6, f32[1,128]{1,0:T(1,128)} %bitcast.7, ...), custom_call_target="tpu_custom_call" | custom-call | tf_op jit(solution)/shard_map/substep/pallas_call | solution.py:428
  47.9 1.1 %copy.11 = f32[3,16,64,128]{3,2,1,0:T(8,128)} copy(f32[3,16,64,128]{3,2,1,0:T(8,128)S(1)} %substep.1) | data formatting | bytes 3145728

commit v7 on v6

--- a/solution.py
+++ b/solution.py
@@ -9,7 +9,7 @@
 BF16 = jnp.bfloat16
 F32 = jnp.float32
 
-MSG = 8
+MSG = 4
 NF = 6
 PAD = 8
 WN = 8

time: 49.1 us -> 48.9 us (level)
  no operation moved by 1% of the time
where the time goes in v7:
time: 48.9 us; the launch traced here: 48.8 us
  Pallas kernels  47 us (96%)
  local copies, waits for them, and re-layouts  1.15 us (2%)
  between operations  0.66 us (1%)
    pallas_call x1, Pallas kernels, per_device(): pl.pallas_call(kernel, name='substep', out_shape=jax.ShapeDtypeStruct(adj...  47 us
    unnamed x1, local copies, waits for them, and re-layouts  1.15 us

profile of v7, /device:TPU:1, one launch (start us, length us, event | category | flops | bytes accessed | tf_op | source)
XLA Modules:
  0.0 48.8 jit_solution(8052696064797077021)
XLA Ops:
  0.7 47.0 %substep.1 = f32[3,16,64,128]{3,2,1,0:T(8,128)S(1)} custom-call(f32[3,16,64,128]{3,2,1,0:T(8,128)} %adj_ref.1, f32[3,16,64,128]{3,2,1,0:T(8,128)} %base_ref.1, f32[1,64]{1,0:T(1,128)} %bitcast.4, f32[512,512]{1,0:T(8,128)} %prop_ref.1, s32[1,128]{1,0:T(1,128)} %bitcast.5, f32[1,128]{1,0:T(1,128)} %bitcast.6, f32[1,128]{1,0:T(1,128)} %bitcast.7, ...), custom_call_target="tpu_custom_call" | custom-call | tf_op jit(solution)/shard_map/substep/pallas_call | solution.py:428
  47.6 1.1 %copy.11 = f32[3,16,64,128]{3,2,1,0:T(8,128)} copy(f32[3,16,64,128]{3,2,1,0:T(8,128)S(1)} %substep.1) | data formatting | bytes 3145728
